TPU v7x, 128 devices: a whole 4x4x4 slice. The times are simulated.
128 devices in a mesh: row: 8 (over x, z_hi), col: 16 (over z_lo, y, core).
Axes of the slice: x: 4, y: 4, z: 4 (z_hi: 2, z_lo: 2; z = z_hi * 2 + z_lo), core: 2. Of those that a mesh axis runs over, the one named last changes fastest.
Arguments:
- tokens: bfloat16 [1024, 6144], P('row', 'col'), may hold values from -6 to 6
- w_in: bfloat16 [6144, 24576], P('col', 'row'), may hold values from -0.078125 to 0.078125
- w_out: bfloat16 [24576, 6144], P('row', 'col'), may hold values from -0.0390625 to 0.0390625
- out_grad: bfloat16 [1024, 6144], P('row', 'col'), may hold values from -6 to 6
Outputs:
- mlp_out: bfloat16 [1024, 6144], P('row', 'col')
- in_grad: bfloat16 [1024, 6144], P('row', 'col')
- w_in_grad: float32 [6144, 24576], P('col', 'row')
- w_out_grad: float32 [24576, 6144], P('row', 'col')
All inputs are finite; a program needn't handle non-finite values.
Results may differ from a plain program's by a relative error of at most 0.005.
Values may be sent and summed in bfloat16 or wider, within the bound.
A program may use at most 128 MiB of HBM per device.

v0:
```python
import jax
import jax.numpy as jnp
from jax import lax
from jax.sharding import PartitionSpec as P

sqrt_half = 0.7071067811865476
inv_root = 0.3989422804014327


def gelu_value(value):
    return 0.5 * value * (1.0 + jax.scipy.special.erf(value * sqrt_half))


def gelu_slope(value):
    return (
        0.5 * (1.0 + jax.scipy.special.erf(value * sqrt_half))
        + value * jnp.exp(-0.5 * value * value) * inv_root
    )


def contract(left, right, left_dim, right_dim):
    return lax.dot_general(
        left, right, (((left_dim,), (right_dim,)), ((), ())), preferred_element_type=jnp.float32
    )


def on_device(tokens, w_in, w_out, out_grad):
    x_all = lax.all_gather(tokens, "row", axis=0, tiled=True)
    preact = lax.psum_scatter(
        jnp.dot(x_all, w_in, preferred_element_type=jnp.float32),
        "col",
        scatter_dimension=0,
        tiled=True,
    )
    hidden = gelu_value(preact).astype(jnp.bfloat16)
    out_terms = jnp.dot(
        lax.all_gather(hidden, "col", axis=0, tiled=True), w_out, preferred_element_type=jnp.float32
    )
    mlp_out = lax.psum_scatter(out_terms, "row", scatter_dimension=0, tiled=True).astype(
        jnp.bfloat16
    )
    grad_all = lax.all_gather(out_grad, "row", axis=0, tiled=True)
    hidden_grad = lax.psum_scatter(
        contract(grad_all, w_out, 1, 1), "col", scatter_dimension=0, tiled=True
    )
    preact_grad = (hidden_grad * gelu_slope(preact)).astype(jnp.bfloat16)
    w_out_grad = contract(lax.all_gather(hidden, "col", axis=0, tiled=True), grad_all, 0, 0)
    piece = lax.all_gather(preact_grad, "col", axis=0, tiled=True)
    in_terms = contract(piece, w_in, 1, 1)
    in_terms, w_in_grad = (in_terms, contract(x_all, piece, 0, 0))
    in_grad = lax.psum_scatter(in_terms, "row", scatter_dimension=0, tiled=True).astype(
        jnp.bfloat16
    )
    return (mlp_out, in_grad, w_in_grad, w_out_grad)


def solution(mesh):
    in_specs = (P("row", "col"), P("col", "row"), P("row", "col"), P("row", "col"))
    out_specs = (P("row", "col"), P("row", "col"), P("col", "row"), P("row", "col"))
    return jax.shard_map(
        on_device, mesh=mesh, in_specs=in_specs, out_specs=out_specs, check_vma=False
    )
```

profile of v0, /device:TPU:0, one launch (start us, length us, event | category | flops | bytes accessed | tf_op | source)
XLA Modules:
  0.0 483.7 jit_solution(9317116042536726726)
XLA Ops:
  7.2 0.0 reduce-scatter.9.cloned.1.call-start
  7.2 36.5 %all_gather.15 = bf16[1024,384]{1,0:T(8,128)(2,1)S(1)} all-gather(bf16[128,384]{1,0:T(8,128)(2,1)} %param.7), channel_id=1, replica_groups=mesh['row'=8,'col'=16] {'row'}, dimensions={0}, use_global_device_ids=true | all-gather | bytes 884736 | tf_op jit(solution)/shard_map/all_gather | solution.py:42
  43.7 1.0 copy-done.1
  44.7 6.3 %fusion.8 = f32[1024,3072]{1,0:T(8,128)} fusion(bf16[1024,384]{1,0:T(8,128)(2,1)S(1)} %all_gather.15, bf16[3072,384]{1,0:T(8,128)(2,1)S(1)} %copy-done), kind=kOutput, calls=%fused_computation.12 | convolution fusion | flops 2415919104 | bytes 15728640 | tf_op jit(solution)/shard_map/dot_general | solution.py:22
  51.0 0.0 reduce-scatter.9.cloned.1.call-update
  51.0 0.0 reduce-scatter.5.cloned.1.call-start
  51.1 0.8 copy-done.3
  51.9 89.0 %all_gather.13 = bf16[1024,384]{1,0:T(8,128)(2,1)S(1)} all-gather(bf16[128,384]{1,0:T(8,128)(2,1)S(1)} %copy-done.3), channel_id=1, replica_groups=mesh['row'=8,'col'=16] {'row'}, dimensions={0}, use_global_device_ids=true | all-gather | bytes 884736 | tf_op jit(solution)/shard_map/all_gather | solution.py:28
  140.9 7.9 %fusion.6 = f32[1024,3072]{1,0:T(8,128)} fusion(bf16[1024,384]{1,0:T(8,128)(2,1)S(1)} %all_gather.13, bf16[384,3072]{1,0:T(8,128)(2,1)} %param.5), kind=kOutput, calls=%fused_computation.10 | convolution fusion | flops 2415919104 | bytes 15728640 | tf_op jit(solution)/shard_map/dot_general | solution.py:30
  148.8 0.0 reduce-scatter.5.cloned.1.call-update
  148.9 0.0 all-gather.3.cloned.1.call-start
  148.9 0.0 reduce-scatter.9.cloned.1.call-done
  148.9 81.8 %reduce-scatter.5.cloned.1.call-done = f32[64,3072]{1,0:T(8,128)} async-done(((f32[1024,3072]{1,0:T(8,128)}), f32[64,3072]{1,0:T(8,128)}) %reduce-scatter.5.cloned.1.call-update) | async-done | bytes 786448 | tf_op jit(solution)/shard_map/reduce_scatter | solution.py:29
  230.7 2.6 fusion.5
  233.4 0.0 all-gather.3.cloned.1.call-update
  233.4 0.0 all-gather.5.cloned.1.call-start
  233.4 0.5 all-gather.5.cloned.1.call-update
  234.0 0.0 reduce-scatter.7.cloned.1.call-start
  234.0 40.8 %all-gather.3.cloned.1.call-done = bf16[1024,3072]{1,0:T(8,128)(2,1)} async-done(((bf16[64,3072]{1,0:T(8,128)(2,1)}), bf16[1024,3072]{1,0:T(8,128)(2,1)}) %all-gather.3.cloned.1.call-update) | async-done | bytes 6291472 | tf_op jit(solution)/shard_map/all_gather | solution.py:37
  274.8 6.6 %fusion.7 = f32[1024,384]{1,0:T(8,128)} fusion(bf16[1024,3072]{1,0:T(8,128)(2,1)} %all-gather.3.cloned.1.call-done, bf16[3072,384]{1,0:T(8,128)(2,1)S(1)} %copy-done), kind=kOutput, calls=%fused_computation.11 | convolution fusion | flops 2415919104 | bytes 10223616 | tf_op jit(solution)/shard_map/dot_general | solution.py:36
  281.4 0.0 reduce-scatter.7.cloned.1.call-update
  281.4 0.2 reduce-scatter.11.cloned.1.call-start
  281.7 38.4 %all-gather.5.cloned.1.call-done = bf16[1024,3072]{1,0:T(8,128)(2,1)} async-done(((bf16[64,3072]{1,0:T(8,128)(2,1)}), bf16[1024,3072]{1,0:T(8,128)(2,1)}) %all-gather.5.cloned.1.call-update) | async-done | bytes 6291472 | tf_op jit(solution)/shard_map/all_gather | solution.py:48
  320.1 8.0 %fusion.9 = f32[1024,384]{1,0:T(8,128)} fusion(bf16[1024,3072]{1,0:T(8,128)(2,1)} %all-gather.5.cloned.1.call-done, bf16[384,3072]{1,0:T(8,128)(2,1)} %param.5), kind=kOutput, calls=%fused_computation.13 | convolution fusion | flops 2415919104 | bytes 10223616 | tf_op jit(solution)/shard_map/dot_general | solution.py:22
  328.1 0.0 reduce-scatter.11.cloned.1.call-update
  328.1 8.4 %convolution_bitcast_fusion = f32[384,3072]{0,1:T(8,128)} fusion(bf16[1024,3072]{1,0:T(8,128)(2,1)} %all-gather.5.cloned.1.call-done, bf16[1024,384]{1,0:T(8,128)(2,1)S(1)} %all_gather.13), kind=kOutput, calls=%fused_computation | convolution fusion | flops 2415919104 | bytes 11796480 | tf_op jit(solution)/shard_map/dot_general | solution.py:22
  336.6 6.1 %copy.8 = f32[384,3072]{1,0:T(8,128)} copy(f32[384,3072]{0,1:T(8,128)} %convolution_bitcast_fusion) | data formatting | bytes 9437184
  342.7 8.5 %fusion.10 = f32[3072,384]{1,0:T(8,128)} fusion(bf16[1024,3072]{1,0:T(8,128)(2,1)} %all-gather.3.cloned.1.call-done, bf16[1024,384]{1,0:T(8,128)(2,1)S(1)} %copy-done.2), kind=kOutput, calls=%fused_computation.14 | convolution fusion | flops 2415919104 | bytes 11796480 | tf_op jit(solution)/shard_map/dot_general | solution.py:22
  351.2 47.5 %reduce-scatter.7.cloned.1.call-done = f32[128,384]{1,0:T(8,128)} async-done(((f32[1024,384]{1,0:T(8,128)}), f32[128,384]{1,0:T(8,128)}) %reduce-scatter.7.cloned.1.call-update) | async-done | bytes 196624 | tf_op jit(solution)/shard_map/reduce_scatter | solution.py:39
  398.7 1.6 convert_element_type.13
  400.3 75.0 %reduce-scatter.11.cloned.1.call-done = f32[128,384]{1,0:T(8,128)} async-done(((f32[1024,384]{1,0:T(8,128)}), f32[128,384]{1,0:T(8,128)}) %reduce-scatter.11.cloned.1.call-update) | async-done | bytes 196624 | tf_op jit(solution)/shard_map/reduce_scatter | solution.py:51
  475.3 1.6 convert_element_type.15
  (6 shorter events, 0.0 us)
Async XLA Ops:
  7.2 37.5 %copy-start = (bf16[3072,384]{1,0:T(8,128)(2,1)S(1)}, bf16[3072,384]{1,0:T(8,128)(2,1)}, u32[]{:S(2)}) copy-start(bf16[3072,384]{1,0:T(8,128)(2,1)} %param.6) | copy-start | bytes 7077892
  7.2 141.8 %reduce-scatter.9.cloned.1.call-start = ((), (), s32[]{:S(2)}) async-start(), calls=%async_computation.7 | async-start | bytes 13369344 | tf_op jit(solution)/shard_map/reduce_scatter | solution.py:43
  43.7 1.0 copy-start.1
  51.0 0.9 copy-start.3
  51.0 179.7 %reduce-scatter.5.cloned.1.call-start = ((), (), s32[]{:S(2)}) async-start(), calls=%async_computation.4 | async-start | bytes 13369344 | tf_op jit(solution)/shard_map/reduce_scatter | solution.py:29
  148.9 125.9 %all-gather.3.cloned.1.call-start = ((), (), s32[]{:S(2)}) async-start(), calls=%async_computation.5 | async-start | bytes 6684672 | tf_op jit(solution)/shard_map/all_gather | solution.py:37
  233.4 86.7 %all-gather.5.cloned.1.call-start = ((), (), s32[]{:S(2)}) async-start(), calls=%async_computation.8 | async-start | bytes 6684672 | tf_op jit(solution)/shard_map/all_gather | solution.py:48
  234.0 164.8 %reduce-scatter.7.cloned.1.call-start = ((), (), s32[]{:S(2)}) async-start(), calls=%async_computation.6 | async-start | bytes 1769472 | tf_op jit(solution)/shard_map/reduce_scatter | solution.py:39
  281.4 193.9 %reduce-scatter.11.cloned.1.call-start = ((), (), s32[]{:S(2)}) async-start(), calls=%async_computation.9 | async-start | bytes 1769472 | tf_op jit(solution)/shard_map/reduce_scatter | solution.py:51
  336.6 6.1 %copy-start.2 = (bf16[1024,384]{1,0:T(8,128)(2,1)S(1)}, bf16[1024,384]{1,0:T(8,128)(2,1)}, u32[]{:S(2)}) copy-start(bf16[1024,384]{1,0:T(8,128)(2,1)} %copy-done.1) | copy-start | bytes 2359300
Sparse Core Ops, SparseCore 0:
  51.2 87.9 reduce-scatter.8
  149.0 81.6 reduce-scatter.4
  233.5 41.2 all-gather.2
  276.9 43.1 all-gather.4
  323.7 75.0 reduce-scatter.6
  402.4 72.9 reduce-scatter.10
where the time goes:
time: 484 us
  waiting for transfers between devices  284 us (59%)
  blocking collectives  125 us (26%)
  matrix products  45.9 us (9%)
  between operations  14.1 us (3%)
  local copies, waits for them, and re-layouts  7.91 us (2%)
  other arithmetic  5.78 us (1%)
    all_gather x1, blocking collectives, on_device(): x_all = lax.all_gather(tokens, 'row', axis=0, tiled=True)  89 us
    reduce_scatter x1, waiting for transfers between devices, on_device(): lax.psum_scatter(jnp.dot(x_all, w_in, preferred_element_type=jnp.float32)...  81.8 us
    reduce_scatter x1, waiting for transfers between devices, on_device(): lax.psum_scatter(in_terms, 'row', scatter_dimension=0, tiled=True)  75 us
    reduce_scatter x1, waiting for transfers between devices, on_device(): lax.psum_scatter(out_terms, 'row', scatter_dimension=0, tiled=True)  47.5 us
    all_gather x1, waiting for transfers between devices, on_device(): lax.all_gather(hidden, 'col', axis=0, tiled=True)  40.8 us
    all_gather x1, waiting for transfers between devices, on_device(): piece = lax.all_gather(preact_grad, 'col', axis=0, tiled=True)  38.4 us
    all_gather x1, blocking collectives, on_device(): grad_all = lax.all_gather(out_grad, 'row', axis=0, tiled=True)  36.5 us
    dot_general x4, matrix products, contract(): lax.dot_general(left, right, (((left_dim,), (right_dim,)), ((), ())), pre...  31.3 us
  transfers between devices with their start and end apart: 6, of which 5 were waited for; matrix products, arithmetic and copies ran while one was open for 10% of the time, Pallas kernels for 0%

commit v1 on v0

v1 whole, which is shorter than its diff:
```python
import jax
import jax.numpy as jnp
from jax import lax
from jax.experimental import pallas as pl
from jax.experimental.pallas import tpu as pltpu
from jax.sharding import PartitionSpec as P

MESH = pl.DeviceIdType.MESH
f32, bf16 = jnp.float32, jnp.bfloat16
sqrt_half = 0.7071067811865476
inv_root = 0.3989422804014327

ROWS = 8
TOK = 128
DL = 384
DC = 768
FL = 3072
FH = 1536
NCH = 8
B = TOK // NCH
C = B * ROWS
WA, WB = 1024, 512
HA, HB = WA // 2, WB // 2
STAGES = 13

(AGZ, AGX, AGC, A_REL, A_DIR, A_SUM, A_Z, B_Z, B_REL, B_DIR, B_SUM, GA_Z, GA_1, GA_2, GB_1, GB_2, GB_Z, GC, RX, RZ) = range(20)
KINDS = 20


def kernel(
    tok, dy, w_in, w_out,
    mlp, ing, wig, wog,
    xall, wih, woh, winv, woutv, part,
    a_rel, a_dir, a_sum, a_out, a_z, b_z, b_rel, b_dir, b_sum,
    hid, oc, xr, xs, zr, g_in, g_out,
    ssem, rsem, wsem, lsem,
):
    row, col = lax.axis_index("row"), lax.axis_index("col")
    x, zh = row // 2, row % 2
    zl, y, core = col // 8, (col // 2) % 4, col % 2
    other = 1 - core

    def dev(dx=0, dzh=0, dzl=0, dyy=0, dc=0):
        return (
            ((x + dx) % 4) * 2 + (zh + dzh) % 2,
            (((zl + dzl) % 2) * 4 + (y + dyy) % 4) * 2 + (core + dc) % 2,
        )

    XP, XM, XO = dev(dx=1), dev(dx=3), dev(dx=2)
    ZH, ZL = dev(dzh=1), dev(dzl=1)
    YP, YM = dev(dyy=1), dev(dyy=3)
    CO = dev(dc=1)
    yr, yl, yo = (y + 1) % 4, (y + 3) % 4, (y + 2) % 4

    def send(src, dst, c, kind, to):
        pltpu.make_async_remote_copy(
            src_ref=src, dst_ref=dst, send_sem=ssem.at[c, kind], recv_sem=rsem.at[c, kind],
            device_id=to, device_id_type=MESH,
        ).start()

    def got(view, c, kind):
        pltpu.make_async_copy(view, view, rsem.at[c, kind]).wait()

    def sent(view, c, kind):
        pltpu.make_async_copy(view, view, ssem.at[c, kind]).wait()

    def ds(i, size):
        return pl.ds(pl.multiple_of(i * size, size), size)

    barrier = pltpu.get_barrier_semaphore()
    for d in (XP, XM, XO, ZH, ZL, YP, YM, CO):
        pl.semaphore_signal(barrier, 1, device_id=d, device_id_type=MESH)
    pl.semaphore_wait(barrier, 8)

    swaps = [
        pltpu.make_async_remote_copy(
            src_ref=w_in.at[:, ds(other, FH)], dst_ref=wih.at[pl.ds(DL, DL), :],
            send_sem=wsem.at[0], recv_sem=wsem.at[1], device_id=CO, device_id_type=MESH,
        ),
        pltpu.make_async_remote_copy(
            src_ref=w_out.at[ds(other, FH), :], dst_ref=woh.at[:, pl.ds(DL, DL)],
            send_sem=wsem.at[2], recv_sem=wsem.at[3], device_id=CO, device_id_type=MESH,
        ),
    ]
    locals_ = [
        pltpu.make_async_copy(w_in.at[:, ds(core, FH)], wih.at[pl.ds(0, DL), :], lsem.at[0]),
        pltpu.make_async_copy(w_out.at[ds(core, FH), :], woh.at[:, pl.ds(0, DL)], lsem.at[1]),
        pltpu.make_async_copy(w_in, winv, lsem.at[2]),
        pltpu.make_async_copy(w_out, woutv, lsem.at[3]),
    ]
    results = [
        pltpu.make_async_copy(g_out, wog, lsem.at[4]),
        pltpu.make_async_copy(g_in, wig, lsem.at[5]),
    ]

    def s0(c):
        mine = ds(row, B)
        xall[c, 0, mine, 0:DL] = tok[ds(c, B), :]
        xall[c, 1, mine, 0:DL] = dy[ds(c, B), :]
        view = xall.at[c, :, mine, 0:DL]
        send(view, view, c, AGZ, ZH)
        for to in (XP, XM, XO):
            send(view, view, c, AGX, to)

    def s1(c):
        view = xall.at[c, :, ds(x * 2 + 1 - zh, B), 0:DL]
        got(view, c, AGZ)
        for to in (XP, XM, XO):
            send(view, view, c, AGX, to)

    def s2(c):
        got(xall.at[c, :, 0 : 6 * B, 0:DL], c, AGX)
        send(xall.at[c, :, :, 0:DL], xall.at[c, :, :, DL:DC], c, AGC, CO)

    def y_rows(d, rows, off):
        return pl.ds(pl.multiple_of(d * rows + off, B), rows)

    def y_send(c, rows, off, c0, h, rel, direct, krel, kdir):
        first, second = pl.ds(c0, h), pl.ds(c0 + h, h)
        send(part.at[c, :, y_rows(yo, rows, off), first], rel.at[c, 0], c, krel, YP)
        send(part.at[c, :, y_rows(yo, rows, off), second], rel.at[c, 1], c, krel, YM)
        send(part.at[c, :, y_rows(yr, rows, off), second], direct.at[c, 0], c, kdir, YP)
        send(part.at[c, :, y_rows(yl, rows, off), first], direct.at[c, 1], c, kdir, YM)

    def y_relay(c, rows, off, c0, h, rel, total, krel, ksum):
        got(rel.at[c], c, krel)
        for i, (d, to) in enumerate(((yr, YP), (yl, YM))):
            place = (c, slice(None), y_rows(d, rows, off), pl.ds(c0 + i * h, h))
            part[place] = (part[place].astype(f32) + rel[c, i].astype(f32)).astype(bf16)
            send(part.at[place], total.at[c, i], c, ksum, to)

    def y_total(c, rows, off, sub, c0, h, direct, total, i):
        own = part[c, :, pl.ds(pl.multiple_of(y * rows + off + sub, B), B), pl.ds(c0 + i * h, h)]
        at = pl.ds(pl.multiple_of(sub, B), B)
        return own.astype(f32) + direct[c, 1 - i, :, at, :].astype(f32) + total[c, i, :, at, :].astype(f32)

    off_b = zl * (4 * B)
    a_mine, b_mine = ds(y * 2 + zl, B), ds(zl * 4 + y, B)

    def s3(c):
        @pl.when(c == 0)
        def _():
            for copy in locals_[:2]:
                copy.wait()
            for copy in swaps:
                copy.wait_recv()

        got(xall.at[c, :, :, DL:DC], c, AGC)

        @pl.loop(0, FH // 256)
        def _(j):
            cols = ds(j, 256)
            part[c, 0, :, cols] = jnp.dot(
                xall[c, 0], wih[:, cols], preferred_element_type=f32
            ).astype(bf16)
            part[c, 1, :, cols] = lax.dot_general(
                xall[c, 1], woh[cols, :], (((1,), (1,)), ((), ())), preferred_element_type=f32
            ).astype(bf16)

        y_send(c, 2 * B, 0, 0, HA, a_rel, a_dir, A_REL, A_DIR)
        send(part.at[c, :, ds(1 - zl, 4 * B), WA:FH], b_z.at[c], c, B_Z, ZL)

    def s4(c):
        y_relay(c, 2 * B, 0, 0, HA, a_rel, a_sum, A_REL, A_SUM)
        got(b_z.at[c], c, B_Z)
        place = (c, slice(None), ds(zl, 4 * B), slice(WA, FH))
        part[place] = (part[place].astype(f32) + b_z[c].astype(f32)).astype(bf16)
        y_send(c, B, off_b, WA, HB, b_rel, b_dir, B_REL, B_DIR)

    def s5(c):
        got(a_dir.at[c], c, A_DIR)
        got(a_sum.at[c], c, A_SUM)
        for i in range(2):
            a_out[c, :, :, i * HA : (i + 1) * HA] = y_total(
                c, 2 * B, 0, (1 - zl) * B, 0, HA, a_dir, a_sum, i
            ).astype(bf16)
        send(a_out.at[c], a_z.at[c], c, A_Z, ZL)
        y_relay(c, B, off_b, WA, HB, b_rel, b_sum, B_REL, B_SUM)

    def unit(c, rows, c0, h, pre, grad):
        half_erf = 0.5 * (1.0 + lax.erf(pre * sqrt_half))
        hid[core, c, 0, rows, c0 : c0 + h] = (pre * half_erf).astype(bf16)
        slope = half_erf + pre * jnp.exp(-0.5 * pre * pre) * inv_root
        hid[core, c, 1, rows, c0 : c0 + h] = (grad * slope).astype(bf16)

    def s6(c):
        got(a_z.at[c], c, A_Z)
        for i in range(2):
            both = y_total(c, 2 * B, 0, zl * B, 0, HA, a_dir, a_sum, i)
            both = both + a_z[c, :, :, i * HA : (i + 1) * HA].astype(f32)
            unit(c, a_mine, i * HA, HA, both[0], both[1])
        view = hid.at[core, c, :, a_mine, 0:WA]
        send(view, view, c, GA_Z, ZL)
        got(b_dir.at[c], c, B_DIR)
        got(b_sum.at[c], c, B_SUM)
        for i in range(2):
            both = y_total(c, B, off_b, 0, WA, HB, b_dir, b_sum, i)
            unit(c, b_mine, WA + i * HB, HB, both[0], both[1])
        view = hid.at[core, c, :, b_mine, WA:FH]
        send(view, view, c, GB_1, YP)
        send(view, view, c, GB_1, YM)

    def y_forward(c, rows, off, c0, h, kind):
        for i, (d, to) in enumerate(((yl, YP), (yr, YM))):
            view = hid.at[core, c, :, y_rows(d, rows, off), pl.ds(c0 + i * h, h)]
            send(view, view, c, kind, to)

    def s7(c):
        got(hid.at[core, c, :, ds(y * 2 + 1 - zl, B), 0:WA], c, GA_Z)
        view = hid.at[core, c, :, ds(y, 2 * B), 0:WA]
        send(view, view, c, GA_1, YP)
        send(view, view, c, GA_1, YM)
        got(hid.at[core, c, :, 0 : 2 * B, WA:FH], c, GB_1)
        y_forward(c, B, off_b, WA, HB, GB_2)

    def s8(c):
        got(hid.at[core, c, :, 0 : 4 * B, 0:WA], c, GA_1)
        y_forward(c, 2 * B, 0, 0, HA, GA_2)
        got(hid.at[core, c, :, 0:B, WA:FH], c, GB_2)
        view = hid.at[core, c, :, ds(zl, 4 * B), WA:FH]
        send(view, view, c, GB_Z, ZL)

    def s9(c):
        got(hid.at[core, c, :, 0 : 2 * B, 0:WA], c, GA_2)
        got(hid.at[core, c, :, 0 : 4 * B, WA:FH], c, GB_Z)
        send(hid.at[core, c], hid.at[core, c], c, GC, CO)

    def s10(c):
        @pl.when(c == 0)
        def _():
            for copy in locals_[2:]:
                copy.wait()

        got(hid.at[other, c], c, GC)
        for k in range(2):
            units = pl.ds(k * FH, FH)
            out = jnp.dot(hid[k, c, 0], woutv[units, :], preferred_element_type=f32)
            back = lax.dot_general(
                hid[k, c, 1], winv[:, units], (((1,), (1,)), ((), ())), preferred_element_type=f32
            )
            if k == 0:
                oc[c, 0], oc[c, 1] = out, back
            else:
                oc[c, 0] += out
                oc[c, 1] += back
        for i, (d, to) in enumerate((((x + 1) % 4, XP), ((x + 3) % 4, XM), ((x + 2) % 4, XO))):
            send(oc.at[c, :, ds(d, 2 * B), :], xr.at[c, i], c, RX, to)

        @pl.when(c % 2 == 1)
        def _():
            pair = pl.ds(c - 1, 2)
            tn = (((0,), (0,)), ((), ()))
            for k in range(2):

                @pl.loop(0, FH // 256)
                def _(j):
                    units = hid[k, pair, 0, :, ds(j, 256)].reshape(2 * C, 256)
                    down = xall[pair, 1, :, 0:DL].reshape(2 * C, DL)
                    g_out[ds(k * (FH // 256) + j, 256), :] += lax.dot_general(
                        units, down, tn, preferred_element_type=f32
                    )

            @pl.when(c == NCH - 1)
            def _():
                results[0].start()

            for k in range(2):

                @pl.loop(0, FH // 256)
                def _(j):
                    units = hid[k, pair, 1, :, ds(j, 256)].reshape(2 * C, 256)
                    up = xall[pair, 0, :, 0:DL].reshape(2 * C, DL)
                    g_in[:, ds(k * (FH // 256) + j, 256)] += lax.dot_general(
                        up, units, tn, preferred_element_type=f32
                    )

            @pl.when(c == NCH - 1)
            def _():
                results[1].start()

    def x_total(c, z):
        at = ds(z, B)
        total = oc[c, :, pl.ds(pl.multiple_of(x * (2 * B) + z * B, B), B), :]
        for i in range(3):
            total = total + xr[c, i, :, at, :]
        return total

    def s11(c):
        got(xr.at[c], c, RX)
        xs[c] = x_total(c, 1 - zh)
        send(xs.at[c], zr.at[c], c, RZ, ZH)

    def s12(c):
        got(zr.at[c], c, RZ)
        total = x_total(c, zh) + zr[c]
        mlp[ds(c, B), :] = total[0].astype(bf16)
        ing[ds(c, B), :] = total[1].astype(bf16)
        sent(xall.at[c, :, 0:B, 0:DL], c, AGZ)
        sent(xall.at[c, :, 0 : 6 * B, 0:DL], c, AGX)
        sent(xall.at[c, :, :, 0:DL], c, AGC)
        for buf, kind in (
            (a_rel, A_REL), (a_dir, A_DIR), (a_sum, A_SUM), (a_z, A_Z),
            (b_z, B_Z), (b_rel, B_REL), (b_dir, B_DIR), (b_sum, B_SUM), (xr, RX), (zr, RZ),
        ):
            sent(buf.at[c], c, kind)
        for rows, cols, kind in (
            (B, slice(0, WA), GA_Z), (4 * B, slice(0, WA), GA_1), (2 * B, slice(0, WA), GA_2),
            (2 * B, slice(WA, FH), GB_1), (B, slice(WA, FH), GB_2), (4 * B, slice(WA, FH), GB_Z),
        ):
            sent(hid.at[core, c, :, 0:rows, cols], c, kind)
        sent(hid.at[core, c], c, GC)

    for copy in locals_:
        copy.start()
    for copy in swaps:
        copy.start()
    g_in[...] = jnp.zeros_like(g_in)
    g_out[...] = jnp.zeros_like(g_out)

    order = (
        (12, s12), (11, s11), (9, s9), (8, s8), (7, s7), (6, s6), (5, s5), (4, s4),
        (2, s2), (1, s1), (0, s0), (3, s3), (10, s10),
    )

    @pl.loop(0, NCH + STAGES - 1)
    def _(t):
        for stage, work in order:

            @pl.when((t >= stage) & (t < stage + NCH))
            def _(stage=stage, work=work):
                work(t - stage)

    for copy in results:
        copy.wait()
    for copy in swaps:
        copy.wait_send()


def on_device(tokens, w_in, w_out, out_grad):
    vmem, anywhere = pl.BlockSpec(memory_space=pltpu.VMEM), pl.BlockSpec(memory_space=pl.ANY)
    scratch = [
        ((NCH, 2, C, DC), bf16),
        ((DC, FH), bf16),
        ((FH, DC), bf16),
        ((DL, FL), bf16),
        ((FL, DL), bf16),
        ((NCH, 2, C, FH), bf16),
        ((NCH, 2, 2, 2 * B, HA), bf16),
        ((NCH, 2, 2, 2 * B, HA), bf16),
        ((NCH, 2, 2, 2 * B, HA), bf16),
        ((NCH, 2, B, WA), bf16),
        ((NCH, 2, B, WA), bf16),
        ((NCH, 2, 4 * B, WB), bf16),
        ((NCH, 2, 2, B, HB), bf16),
        ((NCH, 2, 2, B, HB), bf16),
        ((NCH, 2, 2, B, HB), bf16),
        ((2, NCH, 2, C, FH), bf16),
        ((NCH, 2, C, DL), f32),
        ((NCH, 3, 2, 2 * B, DL), f32),
        ((NCH, 2, B, DL), f32),
        ((NCH, 2, B, DL), f32),
        ((DL, FL), f32),
        ((FL, DL), f32),
    ]
    return pl.pallas_call(
        kernel,
        out_shape=(
            jax.ShapeDtypeStruct((TOK, DL), bf16),
            jax.ShapeDtypeStruct((TOK, DL), bf16),
            jax.ShapeDtypeStruct((DL, FL), f32),
            jax.ShapeDtypeStruct((FL, DL), f32),
        ),
        in_specs=[vmem, vmem, anywhere, anywhere],
        out_specs=(vmem, vmem, anywhere, anywhere),
        scratch_shapes=[pltpu.VMEM(shape, dtype) for shape, dtype in scratch]
        + [
            pltpu.SemaphoreType.DMA((NCH, KINDS)),
            pltpu.SemaphoreType.DMA((NCH, KINDS)),
            pltpu.SemaphoreType.DMA((4,)),
            pltpu.SemaphoreType.DMA((6,)),
        ],
        compiler_params=pltpu.CompilerParams(
            collective_id=0, has_side_effects=True, vmem_limit_bytes=63 * 2**20
        ),
    )(tokens, out_grad, w_in, w_out)


def solution(mesh):
    in_specs = (P("row", "col"), P("col", "row"), P("row", "col"), P("row", "col"))
    out_specs = (P("row", "col"), P("row", "col"), P("col", "row"), P("row", "col"))
    return jax.shard_map(
        on_device, mesh=mesh, in_specs=in_specs, out_specs=out_specs, check_vma=False
    )
```

time: 484 us -> 162 us (0.33)
  waiting for transfers between devices: 284 us -> 0 us
  Pallas kernels: 0 us -> 150 us
  blocking collectives: 125 us -> 0 us
  matrix products: 45.9 us -> 0 us
  between operations: 14.1 us -> 0.64 us
  other arithmetic: 5.78 us -> 0.01 us
    reduce_scatter x4 -> x0, waiting for transfers between devices: 204 us -> none  [the longest x1 81.8 us: on_device(): lax.psum_scatter(jnp.dot(x_all, w_in, preferred_element_type=jnp.float32)...]
    pallas_call x0 -> x1, Pallas kernels: none -> 150 us  [on_device(): pl.pallas_call(kernel, out_shape=(jax.ShapeDtypeStruct((TOK, DL), bf16),...]
    all_gather x2 -> x0, blocking collectives: 125 us -> none  [the longest x1 89 us: on_device(): x_all = lax.all_gather(tokens, 'row', axis=0, tiled=True)]
    all_gather x2 -> x0, waiting for transfers between devices: 79.2 us -> none  [the longest x1 40.8 us: on_device(): lax.all_gather(hidden, 'col', axis=0, tiled=True)]
    dot_general x6 -> x0, matrix products: 45.9 us -> none  [the longest x4 31.3 us: contract(): lax.dot_general(left, right, (((left_dim,), (right_dim,)), ((), ())), pre...]
    convert_element_type x3 -> x0, other arithmetic: 5.78 us -> none  [the longest x1 2.63 us: on_device(): preact_grad = (hidden_grad * gelu_slope(preact)).astype(jnp.bfloat16)]
    unnamed x9 -> x8, local copies, waits for them, and re-layouts: 7.91 us -> 10.5 us
  transfers between devices with their start and end apart: 6 -> 0, of which waited for: 5 -> 0; matrix products, arithmetic and copies ran while one was open for 10% -> 0% of each run, Pallas kernels for 0% -> 0%
where the time goes in v1:
time: 162 us; the launch traced here: 161 us
  Pallas kernels  150 us (93%)
  local copies, waits for them, and re-layouts  10.5 us (6%)
    pallas_call x1, Pallas kernels, on_device(): pl.pallas_call(kernel, out_shape=(jax.ShapeDtypeStruct((TOK, DL), bf16),...  150 us
    unnamed x8, local copies, waits for them, and re-layouts  10.5 us

profile of v1, /device:TPU:0, one launch (start us, length us, event | category | flops | bytes accessed | tf_op | source)
XLA Modules:
  0.0 161.5 jit_solution(3261088654059665591)
XLA Ops:
  0.6 150.3 %shard_map.75 = (bf16[128,384]{1,0:T(8,128)(2,1)}, bf16[128,384]{1,0:T(8,128)(2,1)}, f32[384,3072]{1,0:T(8,128)}, f32[3072,384]{1,0:T(8,128)}) custom-call(bf16[128,384]{1,0:T(8,128)(2,1)} %tok.1, bf16[128,384]{1,0:T(8,128)(2,1)} %dy.1, bf16[384,3072]{1,0:T(8,128)(2,1)} %w_in.1, bf16[3072,384]{1,0:T(8,128)(2,1)} %w_out.1), custom_call_target="tpu_custom_call" | custom-call | tf_op jit(solution)/shard_map/pallas_call | solution.py:365
  151.0 1.5 copy.12
  152.5 0.0 slice-start
  152.5 1.7 %copy.13 = bf16[128,384]{1,0:T(8,128)(2,1)} copy(bf16[128,384]{1,0:T(8,128)(2,1)} %get-tuple-element.9) | data formatting | bytes 196608
  154.2 0.0 slice-start.1
  154.2 5.1 %copy.14 = f32[384,3072]{1,0:T(8,128)} copy(f32[384,3072]{1,0:T(8,128)} %get-tuple-element.10) | data formatting | bytes 9437184
  159.3 0.0 slice-done
  159.3 0.0 slice-done.1
  159.3 2.2 %copy.15 = f32[3072,384]{1,0:T(8,128)} copy(f32[3072,384]{1,0:T(8,128)S(1)} %bitcast.1) | data formatting | bytes 9437184
  (1 shorter events, 0.0 us)
Async XLA Ops:
  152.5 6.8 %slice-start = ((s8[4718592]{0:T(1024)(128)(4,1)}), s8[4194304]{0:T(1024)(128)(4,1)S(1)}, s32[]{:S(2)}) async-start(s8[4718592]{0:T(1024)(128)(4,1)} %bitcast), calls=%async_computation | async-start | bytes 8388608
  154.2 5.1 %slice-start.1 = ((s8[4718592]{0:T(1024)(128)(4,1)}), s8[524288]{0:T(1024)(128)(4,1)S(1)}, s32[]{:S(2)}) async-start(s8[4718592]{0:T(1024)(128)(4,1)} %bitcast), calls=%async_computation.1 | async-start | bytes 1048576

commit v2 on v1

--- a/solution.py
+++ b/solution.py
@@ -21,19 +21,22 @@
 C = B * ROWS
 WA, WB = 1024, 512
 HA, HB = WA // 2, WB // 2
-STAGES = 13
-
-(AGZ, AGX, AGC, A_REL, A_DIR, A_SUM, A_Z, B_Z, B_REL, B_DIR, B_SUM, GA_Z, GA_1, GA_2, GB_1, GB_2, GB_Z, GC, RX, RZ) = range(20)
-KINDS = 20
+HT = TOK // 2
+NEAR = {0: 0, 3: 0, 5: HT, 6: HT}
+FAR = (1, 4)
+STAGES = 10
+
+(AGX, AGC, A_REL, A_DIR, A_SUM, A_Z, B_Z, B_REL, B_DIR, B_SUM, GA_Z, GA_1, GA_2, GB_1, GB_2, GB_Z, GC, RX, RZ) = range(19)
+KINDS = 19
 
 
 def kernel(
     tok, dy, w_in, w_out,
-    mlp, ing, wig, wog,
+    mlp, ing, hid_o, xo,
     xall, wih, woh, winv, woutv, part,
     a_rel, a_dir, a_sum, a_out, a_z, b_z, b_rel, b_dir, b_sum,
-    hid, oc, xr, xs, zr, g_in, g_out,
-    ssem, rsem, wsem, lsem,
+    hid, oc, xr, zs, zr,
+    ssem, rsem, wsem, lsem, hsem,
 ):
     row, col = lax.axis_index("row"), lax.axis_index("col")
     x, zh = row // 2, row % 2
@@ -88,29 +91,35 @@
         pltpu.make_async_copy(w_in, winv, lsem.at[2]),
         pltpu.make_async_copy(w_out, woutv, lsem.at[3]),
     ]
-    results = [
-        pltpu.make_async_copy(g_out, wog, lsem.at[4]),
-        pltpu.make_async_copy(g_in, wig, lsem.at[5]),
-    ]
-
-    def s0(c):
-        mine = ds(row, B)
-        xall[c, 0, mine, 0:DL] = tok[ds(c, B), :]
-        xall[c, 1, mine, 0:DL] = dy[ds(c, B), :]
-        view = xall.at[c, :, mine, 0:DL]
-        send(view, view, c, AGZ, ZH)
-        for to in (XP, XM, XO):
-            send(view, view, c, AGX, to)
-
-    def s1(c):
-        view = xall.at[c, :, ds(x * 2 + 1 - zh, B), 0:DL]
-        got(view, c, AGZ)
-        for to in (XP, XM, XO):
-            send(view, view, c, AGX, to)
+    def near(c, src):
+        half = pl.ds(NEAR[c], HT)
+        send(xall.at[src, :, half, 0:DL], xall.at[c, :, pl.ds(0, HT), 0:DL], c, AGX, XM)
+        send(xall.at[src, :, half, 0:DL], xall.at[c, :, pl.ds(HT, HT), 0:DL], c, AGX, XP)
+
+    def whole(c, src, to):
+        send(xall.at[src, :, :, 0:DL], xall.at[c, :, :, 0:DL], c, AGX, to)
+
+    def gather():
+        xall[NCH - 1, 0, :, 0:DL] = tok[...]
+        xall[NCH - 1, 1, :, 0:DL] = dy[...]
+        near(0, NCH - 1)
+        whole(2, NCH - 1, ZH)
+        whole(1, NCH - 1, XO)
+
+    def forward():
+        got(xall.at[2, :, :, 0:DL], 2, AGX)
+        near(3, 2)
+        whole(4, 2, XO)
+        near(5, 2)
+        near(6, NCH - 1)
 
     def s2(c):
-        got(xall.at[c, :, 0 : 6 * B, 0:DL], c, AGX)
+        @pl.when((c != 2) & (c != NCH - 1))
+        def _():
+            got(xall.at[c, :, :, 0:DL], c, AGX)
+
         send(xall.at[c, :, :, 0:DL], xall.at[c, :, :, DL:DC], c, AGC, CO)
+        pl.when(c == 1)(forward)
 
     def y_rows(d, rows, off):
         return pl.ds(pl.multiple_of(d * rows + off, B), rows)
@@ -243,64 +252,69 @@
             else:
                 oc[c, 0] += out
                 oc[c, 1] += back
-        for i, (d, to) in enumerate((((x + 1) % 4, XP), ((x + 3) % 4, XM), ((x + 2) % 4, XO))):
-            send(oc.at[c, :, ds(d, 2 * B), :], xr.at[c, i], c, RX, to)
-
-        @pl.when(c % 2 == 1)
-        def _():
-            pair = pl.ds(c - 1, 2)
-            tn = (((0,), (0,)), ((), ()))
-            for k in range(2):
-
-                @pl.loop(0, FH // 256)
-                def _(j):
-                    units = hid[k, pair, 0, :, ds(j, 256)].reshape(2 * C, 256)
-                    down = xall[pair, 1, :, 0:DL].reshape(2 * C, DL)
-                    g_out[ds(k * (FH // 256) + j, 256), :] += lax.dot_general(
-                        units, down, tn, preferred_element_type=f32
-                    )
-
-            @pl.when(c == NCH - 1)
-            def _():
-                results[0].start()
-
-            for k in range(2):
-
-                @pl.loop(0, FH // 256)
-                def _(j):
-                    units = hid[k, pair, 1, :, ds(j, 256)].reshape(2 * C, 256)
-                    up = xall[pair, 0, :, 0:DL].reshape(2 * C, DL)
-                    g_in[:, ds(k * (FH // 256) + j, 256)] += lax.dot_general(
-                        up, units, tn, preferred_element_type=f32
-                    )
-
-            @pl.when(c == NCH - 1)
-            def _():
-                results[1].start()
-
-    def x_total(c, z):
-        at = ds(z, B)
-        total = oc[c, :, pl.ds(pl.multiple_of(x * (2 * B) + z * B, B), B), :]
-        for i in range(3):
-            total = total + xr[c, i, :, at, :]
-        return total
+        for copy in keep(c):
+            copy.start()
+        for k, first in NEAR.items():
+
+            @pl.when(c == k)
+            def _(k=k, first=first):
+                for i, to in enumerate((XP, XM)):
+                    dst = xr.at[int(k in (3, 5)), i, :, pl.ds(first, HT), :]
+                    send(oc.at[k, :, pl.ds(i * HT, HT), :], dst, k, RX, to)
+
+        for k in FAR:
+
+            @pl.when(c == k)
+            def _(k=k):
+                send(oc.at[k], xr.at[FAR.index(k), 2], k, RX, XO)
+
+    def keep(c):
+        return [
+            pltpu.make_async_copy(hid.at[0, c], hid_o.at[0, c], hsem.at[c, 0]),
+            pltpu.make_async_copy(hid.at[1, c], hid_o.at[1, c], hsem.at[c, 1]),
+            pltpu.make_async_copy(xall.at[c, :, :, 0:DL], xo.at[c], hsem.at[c, 2]),
+        ]
 
     def s11(c):
-        got(xr.at[c], c, RX)
-        xs[c] = x_total(c, 1 - zh)
-        send(xs.at[c], zr.at[c], c, RZ, ZH)
-
-    def s12(c):
-        got(zr.at[c], c, RZ)
-        total = x_total(c, zh) + zr[c]
-        mlp[ds(c, B), :] = total[0].astype(bf16)
-        ing[ds(c, B), :] = total[1].astype(bf16)
-        sent(xall.at[c, :, 0:B, 0:DL], c, AGZ)
-        sent(xall.at[c, :, 0 : 6 * B, 0:DL], c, AGX)
+        for k, chunks, first in ((4, (3, 4), 0), (5, (5,), HT)):
+
+            @pl.when(c == k)
+            def _(k=k, chunks=chunks, first=first):
+                for chunk in chunks:
+                    got(oc.at[chunk], chunk, RX)
+                half = pl.ds(first, HT)
+                zs[:, half, :] = oc[2, :, half, :] + xr[1, 0, :, half, :] + xr[1, 1, :, half, :] + xr[1, 2, :, half, :]
+                send(zs.at[:, half, :], zr.at[:, half, :], k, RZ, ZH)
+
+        @pl.when(c == NCH - 1)
+        def _():
+            for chunk in (0, 1, 6):
+                got(oc.at[chunk], chunk, RX)
+            for k in (4, 5):
+                got(zr.at[:, 0:HT, :], k, RZ)
+            for i, result in enumerate((mlp, ing)):
+                total = oc[NCH - 1, i] + xr[0, 0, i] + xr[0, 1, i] + xr[0, 2, i] + zr[i]
+                result[...] = total.astype(bf16)
+
+        for copy in keep(c):
+            copy.wait()
+
+        @pl.when(c != NCH - 1)
+        def _():
+            sent(xall.at[c, :, :, 0:DL], c, AGX)
+
+        @pl.when((c != NCH - 1) & (c != 2))
+        def _():
+            sent(oc.at[c], c, RX)
+
+        @pl.when((c == 4) | (c == 5))
+        def _():
+            sent(zr.at[:, 0:HT, :], c, RZ)
+
         sent(xall.at[c, :, :, 0:DL], c, AGC)
         for buf, kind in (
             (a_rel, A_REL), (a_dir, A_DIR), (a_sum, A_SUM), (a_z, A_Z),
-            (b_z, B_Z), (b_rel, B_REL), (b_dir, B_DIR), (b_sum, B_SUM), (xr, RX), (zr, RZ),
+            (b_z, B_Z), (b_rel, B_REL), (b_dir, B_DIR), (b_sum, B_SUM),
         ):
             sent(buf.at[c], c, kind)
         for rows, cols, kind in (
@@ -310,17 +324,13 @@
             sent(hid.at[core, c, :, 0:rows, cols], c, kind)
         sent(hid.at[core, c], c, GC)
 
+    gather()
     for copy in locals_:
         copy.start()
     for copy in swaps:
         copy.start()
-    g_in[...] = jnp.zeros_like(g_in)
-    g_out[...] = jnp.zeros_like(g_out)
-
-    order = (
-        (12, s12), (11, s11), (9, s9), (8, s8), (7, s7), (6, s6), (5, s5), (4, s4),
-        (2, s2), (1, s1), (0, s0), (3, s3), (10, s10),
-    )
+
+    order = ((1, s3), (8, s10), (0, s2), (7, s9), (6, s8), (5, s7), (2, s4), (3, s5), (4, s6), (9, s11))
 
     @pl.loop(0, NCH + STAGES - 1)
     def _(t):
@@ -330,10 +340,25 @@
             def _(stage=stage, work=work):
                 work(t - stage)
 
-    for copy in results:
-        copy.wait()
     for copy in swaps:
         copy.wait_send()
+
+
+TILE = 768
+
+
+def gradients(hid, xo, mlp0, ing0, mlp, ing, wig, wog, xt):
+    @pl.when(pl.program_id(0) == 0)
+    def _():
+        mlp[...] = mlp0[...]
+        ing[...] = ing0[...]
+        xt[...] = xo[:, 0].reshape(NCH * C, DL).T
+
+    units = hid[0, :, 0].reshape(NCH * C, TILE)
+    wog[...] = lax.dot_general(
+        units, xo[:, 1].reshape(NCH * C, DL), (((0,), (0,)), ((), ())), preferred_element_type=f32
+    )
+    wig[...] = jnp.dot(xt[...], hid[0, :, 1].reshape(NCH * C, TILE), preferred_element_type=f32)
 
 
 def on_device(tokens, w_in, w_out, out_grad):
@@ -356,19 +381,17 @@
         ((NCH, 2, 2, B, HB), bf16),
         ((2, NCH, 2, C, FH), bf16),
         ((NCH, 2, C, DL), f32),
-        ((NCH, 3, 2, 2 * B, DL), f32),
-        ((NCH, 2, B, DL), f32),
-        ((NCH, 2, B, DL), f32),
-        ((DL, FL), f32),
-        ((FL, DL), f32),
+        ((2, 3, 2, TOK, DL), f32),
+        ((2, TOK, DL), f32),
+        ((2, TOK, DL), f32),
     ]
-    return pl.pallas_call(
+    mlp, ing, hid, xo = pl.pallas_call(
         kernel,
         out_shape=(
             jax.ShapeDtypeStruct((TOK, DL), bf16),
             jax.ShapeDtypeStruct((TOK, DL), bf16),
-            jax.ShapeDtypeStruct((DL, FL), f32),
-            jax.ShapeDtypeStruct((FL, DL), f32),
+            jax.ShapeDtypeStruct((2, NCH, 2, C, FH), bf16),
+            jax.ShapeDtypeStruct((NCH, 2, C, DL), bf16),
         ),
         in_specs=[vmem, vmem, anywhere, anywhere],
         out_specs=(vmem, vmem, anywhere, anywhere),
@@ -377,12 +400,39 @@
             pltpu.SemaphoreType.DMA((NCH, KINDS)),
             pltpu.SemaphoreType.DMA((NCH, KINDS)),
             pltpu.SemaphoreType.DMA((4,)),
-            pltpu.SemaphoreType.DMA((6,)),
+            pltpu.SemaphoreType.DMA((4,)),
+            pltpu.SemaphoreType.DMA((NCH, 3)),
         ],
         compiler_params=pltpu.CompilerParams(
-            collective_id=0, has_side_effects=True, vmem_limit_bytes=63 * 2**20
+            collective_id=0, has_side_effects=True, vmem_limit_bytes=62 * 2**20
         ),
     )(tokens, out_grad, w_in, w_out)
+    per = FH // TILE
+    small = pl.BlockSpec((TOK, DL), lambda j: (0, 0))
+    return pl.pallas_call(
+        gradients,
+        grid=(2 * per,),
+        out_shape=(
+            jax.ShapeDtypeStruct((TOK, DL), bf16),
+            jax.ShapeDtypeStruct((TOK, DL), bf16),
+            jax.ShapeDtypeStruct((DL, FL), f32),
+            jax.ShapeDtypeStruct((FL, DL), f32),
+        ),
+        in_specs=[
+            pl.BlockSpec((1, NCH, 2, C, TILE), lambda j: (j // per, 0, 0, 0, j % per)),
+            pl.BlockSpec((NCH, 2, C, DL), lambda j: (0, 0, 0, 0)),
+            small,
+            small,
+        ],
+        out_specs=(
+            small,
+            small,
+            pl.BlockSpec((DL, TILE), lambda j: (0, j)),
+            pl.BlockSpec((TILE, DL), lambda j: (j, 0)),
+        ),
+        scratch_shapes=[pltpu.VMEM((DL, NCH * C), bf16)],
+        compiler_params=pltpu.CompilerParams(vmem_limit_bytes=63 * 2**20),
+    )(hid, xo, mlp, ing)
 
 
 def solution(mesh):

time: 162 us -> 135 us (0.83)
  Pallas kernels: 150 us -> 134 us
  local copies, waits for them, and re-layouts: 10.5 us -> 0 us
    pallas_call x1, Pallas kernels: 150 us -> 122 us  [on_device(): pl.pallas_call(kernel, out_shape=(jax.ShapeDtypeStruct((TOK, DL), bf16),...]
    pallas_call x0 -> x1, Pallas kernels: none -> 11.5 us  [on_device(): pl.pallas_call(gradients, grid=(2 * per,), out_shape=(jax.ShapeDtypeStruc...]
    unnamed x8 -> x0, local copies, waits for them, and re-layouts: 10.5 us -> none
where the time goes in v2:
time: 135 us
  Pallas kernels  134 us (99%)
    pallas_call x1, Pallas kernels, on_device(): pl.pallas_call(kernel, out_shape=(jax.ShapeDtypeStruct((TOK, DL), bf16),...  122 us
    pallas_call x1, Pallas kernels, on_device(): pl.pallas_call(gradients, grid=(2 * per,), out_shape=(jax.ShapeDtypeStruc...  11.5 us

profile of v2, /device:TPU:0, one launch (start us, length us, event | category | flops | bytes accessed | tf_op | source)
XLA Modules:
  0.0 134.6 jit_solution(15189300242596274383)
XLA Ops:
  0.6 122.4 %shard_map.75 = (bf16[128,384]{1,0:T(8,128)(2,1)}, bf16[128,384]{1,0:T(8,128)(2,1)}, bf16[2,8,2,128,1536]{4,3,2,1,0:T(8,128)(2,1)}, bf16[8,2,128,384]{3,2,1,0:T(8,128)(2,1)}) custom-call(bf16[128,384]{1,0:T(8,128)(2,1)} %tok.1, bf16[128,384]{1,0:T(8,128)(2,1)} %dy.1, bf16[384,3072]{1,0:T(8,128)(2,1)} %w_in.1, bf16[3072,384]{1,0:T(8,128)(2,1)} %w_out.1), custom_call_target="tpu_custom_call" | custom-call | tf_op jit(solution)/shard_map/pallas_call | solution.py:388
  123.1 11.5 %shard_map.76 = (bf16[128,384]{1,0:T(8,128)(2,1)}, bf16[128,384]{1,0:T(8,128)(2,1)}, f32[384,3072]{1,0:T(8,128)}, f32[3072,384]{1,0:T(8,128)}) custom-call(bf16[2,8,2,128,1536]{4,3,2,1,0:T(8,128)(2,1)} %get-tuple-element.8.hid, bf16[8,2,128,384]{3,2,1,0:T(8,128)(2,1)} %get-tuple-element.9.xo, bf16[128,384]{1,0:T(8,128)(2,1)} %get-tuple-element.10.mlp0, ...), custom_call_target="tpu_custom_call" | custom-call | tf_op jit(solution)/shard_map/pallas_call | solution.py:412

commit v3 on v2

v3 whole, which is shorter than its diff:
```python
import jax
import jax.numpy as jnp
from jax import lax
from jax.experimental import pallas as pl
from jax.experimental.pallas import tpu as pltpu
from jax.sharding import PartitionSpec as P

MESH = pl.DeviceIdType.MESH
f32, bf16 = jnp.float32, jnp.bfloat16
sqrt_half = 0.7071067811865476
inv_root = 0.3989422804014327

ROWS = 8
TOK = 128
DL = 384
DC = 768
FL = 3072
FH = 1536
NCH = 8
B = TOK // NCH
C = B * ROWS
WA, WB = 896, 640
HA, HB = -(-WA // 256) * 128, -(-WB // 256) * 128
HT = TOK // 2
NEAR = {0: 0, 2: 0, 4: HT, 6: HT}
FAR = (5, 3)
OTHER = 1
STAGES = 11

(AGX, AGC, A_REL, A_DIR, A_SUM, A_Z, B_Z, B_REL, B_DIR, B_SUM, GA_Z, GA_1, GA_2, GB_1, GB_2, GB_Z, GC_A, GC_B, RX, RZ) = range(20)
KINDS = 20


def kernel(
    tok, dy, w_in, w_out,
    mlp, ing, hidt_o, pg_o, xt_o, dy_o,
    xall, wih, woh, winv, woutv, part,
    a_rel, a_dir, a_sum, a_out, a_z, b_z, b_rel, b_dir, b_sum,
    hid, hidt, xt, oc, xr, zs, zr,
    ssem, rsem, wsem, lsem, hsem,
):
    row, col = lax.axis_index("row"), lax.axis_index("col")
    x, zh = row // 2, row % 2
    zl, y, core = col // 8, (col // 2) % 4, col % 2
    other = 1 - core

    def dev(dx=0, dzh=0, dzl=0, dyy=0, dc=0):
        return (
            ((x + dx) % 4) * 2 + (zh + dzh) % 2,
            (((zl + dzl) % 2) * 4 + (y + dyy) % 4) * 2 + (core + dc) % 2,
        )

    XP, XM, XO = dev(dx=1), dev(dx=3), dev(dx=2)
    ZH, ZL = dev(dzh=1), dev(dzl=1)
    YP, YM = dev(dyy=1), dev(dyy=3)
    CO = dev(dc=1)
    yr, yl, yo = (y + 1) % 4, (y + 3) % 4, (y + 2) % 4

    def send(src, dst, c, kind, to):
        pltpu.make_async_remote_copy(
            src_ref=src, dst_ref=dst, send_sem=ssem.at[c, kind], recv_sem=rsem.at[c, kind],
            device_id=to, device_id_type=MESH,
        ).start()

    def got(view, c, kind):
        pltpu.make_async_copy(view, view, rsem.at[c, kind]).wait()

    def sent(view, c, kind):
        pltpu.make_async_copy(view, view, ssem.at[c, kind]).wait()

    def ds(i, size):
        return pl.ds(pl.multiple_of(i * size, size), size)

    barrier = pltpu.get_barrier_semaphore()
    for d in (XP, XM, XO, ZH, ZL, YP, YM, CO):
        pl.semaphore_signal(barrier, 1, device_id=d, device_id_type=MESH)
    takes = [
        pltpu.make_async_copy(src, xall.at[NCH - 1, i, :, 0:DL], lsem.at[4 + i]) for i, src in enumerate((tok, dy))
    ]
    for copy in takes:
        copy.start()
    pl.semaphore_wait(barrier, 8)

    swaps = [
        pltpu.make_async_remote_copy(
            src_ref=w_in.at[:, ds(other, FH)], dst_ref=wih.at[pl.ds(DL, DL), :],
            send_sem=wsem.at[0], recv_sem=wsem.at[1], device_id=CO, device_id_type=MESH,
        ),
        pltpu.make_async_remote_copy(
            src_ref=w_out.at[ds(other, FH), :], dst_ref=woh.at[:, pl.ds(DL, DL)],
            send_sem=wsem.at[2], recv_sem=wsem.at[3], device_id=CO, device_id_type=MESH,
        ),
    ]
    locals_ = [
        pltpu.make_async_copy(w_in.at[:, ds(core, FH)], wih.at[pl.ds(0, DL), :], lsem.at[0]),
        pltpu.make_async_copy(w_out.at[ds(core, FH), :], woh.at[:, pl.ds(0, DL)], lsem.at[1]),
        pltpu.make_async_copy(w_in, winv, lsem.at[2]),
        pltpu.make_async_copy(w_out, woutv, lsem.at[3]),
    ]
    def near(c, src):
        half = pl.ds(NEAR[c], HT)
        send(xall.at[src, :, half, 0:DL], xall.at[c, :, pl.ds(0, HT), 0:DL], c, AGX, XM)
        send(xall.at[src, :, half, 0:DL], xall.at[c, :, pl.ds(HT, HT), 0:DL], c, AGX, XP)

    def whole(c, src, to):
        send(xall.at[src, :, :, 0:DL], xall.at[c, :, :, 0:DL], c, AGX, to)

    def gather():
        near(0, NCH - 1)
        whole(OTHER, NCH - 1, ZH)

    def forward():
        got(xall.at[OTHER, :, :, 0:DL], OTHER, AGX)
        near(2, OTHER)
        whole(FAR[1], OTHER, XO)
        near(4, OTHER)
        whole(FAR[0], NCH - 1, XO)
        near(6, NCH - 1)

    def s2(c):
        pl.when(c == OTHER)(forward)

        @pl.when((c != OTHER) & (c != NCH - 1))
        def _():
            got(xall.at[c, :, :, 0:DL], c, AGX)

        send(xall.at[c, :, :, 0:DL], xall.at[c, :, :, DL:DC], c, AGC, CO)

    def y_rows(d, rows, off):
        return pl.ds(pl.multiple_of(d * rows + off, B), rows)

    def y_send(c, rows, off, c0, cut, c1, rel, direct, krel, kdir):
        h = cut - c0
        for i, (half, place) in enumerate(((pl.ds(c0, h), pl.ds(0, h)), (pl.ds(cut, c1 - cut), pl.ds(h, c1 - cut)))):
            send(part.at[c, :, y_rows(yo, rows, off), half], rel.at[c, :, :, place], c, krel, (YP, YM)[i])
            d, to = ((yl, YM), (yr, YP))[i]
            send(part.at[c, :, y_rows(d, rows, off), half], direct.at[c, :, :, place], c, kdir, to)

    def y_relay(c, rows, off, c0, cut, c1, rel, total, krel, ksum):
        got(rel.at[c], c, krel)
        h = cut - c0
        for half, at, d, to in (
            (pl.ds(c0, h), pl.ds(0, h), yr, YP), (pl.ds(cut, c1 - cut), pl.ds(h, c1 - cut), yl, YM),
        ):
            place = (c, slice(None), y_rows(d, rows, off), half)
            part[place] = (part[place].astype(f32) + rel[c, :, :, at].astype(f32)).astype(bf16)
            send(part.at[place], total.at[c, :, :, at], c, ksum, to)

    def y_total(c, rows, off, sub, c0, c1, direct, total):
        own = part[c, :, pl.ds(pl.multiple_of(y * rows + off + sub, B), B), c0:c1]
        at = pl.ds(pl.multiple_of(sub, B), B)
        return own.astype(f32) + direct[c, :, at, :].astype(f32) + total[c, :, at, :].astype(f32)

    off_b = zl * (4 * B)
    route_a = (2 * B, 0, 0, HA, WA)
    route_b = (B, off_b, WA, WA + HB, FH)
    a_mine, b_mine = ds(y * 2 + zl, B), ds(zl * 4 + y, B)

    def s3(c):
        @pl.when(c == 0)
        def _():
            for copy in locals_[:2]:
                copy.wait()
            for copy in swaps:
                copy.wait_recv()

        got(xall.at[c, :, :, DL:DC], c, AGC)

        def products(first, end):
            @pl.loop(first, end)
            def _(j):
                cols = ds(j, 256)
                part[c, 0, :, cols] = jnp.dot(
                    xall[c, 0], wih[:, cols], preferred_element_type=f32
                ).astype(bf16)
                part[c, 1, :, cols] = lax.dot_general(
                    xall[c, 1], woh[cols, :], (((1,), (1,)), ((), ())), preferred_element_type=f32
                ).astype(bf16)

        products(0, -(-WA // 256))
        y_send(c, *route_a, a_rel, a_dir, A_REL, A_DIR)
        products(-(-WA // 256), FH // 256)
        send(part.at[c, :, ds(1 - zl, 4 * B), WA:FH], b_z.at[c], c, B_Z, ZL)

    def s4a(c):
        y_relay(c, *route_a, a_rel, a_sum, A_REL, A_SUM)

    def s4b(c):
        got(b_z.at[c], c, B_Z)
        place = (c, slice(None), ds(zl, 4 * B), slice(WA, FH))
        part[place] = (part[place].astype(f32) + b_z[c].astype(f32)).astype(bf16)
        y_send(c, *route_b, b_rel, b_dir, B_REL, B_DIR)

    def s5a(c):
        got(a_dir.at[c], c, A_DIR)
        got(a_sum.at[c], c, A_SUM)
        a_out[c] = y_total(c, 2 * B, 0, (1 - zl) * B, 0, WA, a_dir, a_sum).astype(bf16)
        send(a_out.at[c], a_z.at[c], c, A_Z, ZL)

    def s5b(c):
        y_relay(c, *route_b, b_rel, b_sum, B_REL, B_SUM)

    def unit(c, rows, c0, c1, both):
        pre, grad = both[0], both[1]
        half_erf = 0.5 * (1.0 + lax.erf(pre * sqrt_half))
        hid[core, c, 0, rows, c0:c1] = (pre * half_erf).astype(bf16)
        slope = half_erf + pre * jnp.exp(-0.5 * pre * pre) * inv_root
        hid[core, c, 1, rows, c0:c1] = (grad * slope).astype(bf16)

    def s6a(c):
        got(a_z.at[c], c, A_Z)
        unit(c, a_mine, 0, WA, y_total(c, 2 * B, 0, zl * B, 0, WA, a_dir, a_sum) + a_z[c].astype(f32))
        view = hid.at[core, c, :, a_mine, 0:WA]
        send(view, view, c, GA_Z, ZL)

    def s6b(c):
        got(b_dir.at[c], c, B_DIR)
        got(b_sum.at[c], c, B_SUM)
        unit(c, b_mine, WA, FH, y_total(c, B, off_b, 0, WA, FH, b_dir, b_sum))
        view = hid.at[core, c, :, b_mine, WA:FH]
        send(view, view, c, GB_1, YP)
        send(view, view, c, GB_1, YM)

    def y_forward(c, rows, off, c0, cut, c1, kind):
        for d, half, to in ((yl, pl.ds(c0, cut - c0), YP), (yr, pl.ds(cut, c1 - cut), YM)):
            view = hid.at[core, c, :, y_rows(d, rows, off), half]
            send(view, view, c, kind, to)

    def s7a(c):
        got(hid.at[core, c, :, ds(y * 2 + 1 - zl, B), 0:WA], c, GA_Z)
        view = hid.at[core, c, :, ds(y, 2 * B), 0:WA]
        send(view, view, c, GA_1, YP)
        send(view, view, c, GA_1, YM)

    def s7b(c):
        got(hid.at[core, c, :, 0 : 2 * B, WA:FH], c, GB_1)
        y_forward(c, *route_b, GB_2)

    def s8a(c):
        got(hid.at[core, c, :, 0 : 4 * B, 0:WA], c, GA_1)
        y_forward(c, *route_a, GA_2)

    def s8b(c):
        got(hid.at[core, c, :, 0:B, WA:FH], c, GB_2)
        view = hid.at[core, c, :, ds(zl, 4 * B), WA:FH]
        send(view, view, c, GB_Z, ZL)

    def s9a(c):
        got(hid.at[core, c, :, 0 : 2 * B, 0:WA], c, GA_2)
        send(hid.at[core, c, :, :, 0:WA], hid.at[core, c, :, :, 0:WA], c, GC_A, CO)

    def s9b(c):
        got(hid.at[core, c, :, 0 : 4 * B, WA:FH], c, GB_Z)
        send(hid.at[core, c, :, :, WA:FH], hid.at[core, c, :, :, WA:FH], c, GC_B, CO)

    def s10(c):
        @pl.when(c == 0)
        def _():
            for copy in locals_[2:]:
                copy.wait()

        got(hid.at[other, c, :, :, 0:WA], c, GC_A)
        got(hid.at[other, c, :, :, WA:FH], c, GC_B)
        for k in range(2):
            units = pl.ds(k * FH, FH)
            out = jnp.dot(hid[k, c, 0], woutv[units, :], preferred_element_type=f32)
            back = lax.dot_general(
                hid[k, c, 1], winv[:, units], (((1,), (1,)), ((), ())), preferred_element_type=f32
            )
            if k == 0:
                oc[c, 0], oc[c, 1] = out, back
            else:
                oc[c, 0] += out
                oc[c, 1] += back
        for k, first in NEAR.items():

            @pl.when(c == k)
            def _(k=k, first=first):
                for i, to in enumerate((XP, XM)):
                    dst = xr.at[int(k in (2, 4)), i, :, pl.ds(first, HT), :]
                    send(oc.at[k, :, pl.ds(i * HT, HT), :], dst, k, RX, to)

        for k in FAR:

            @pl.when(c == k)
            def _(k=k):
                send(oc.at[k], xr.at[FAR.index(k), 2], k, RX, XO)

        @pl.when(c >= 2)
        def _():
            for copy in keep(c - 2):
                copy.wait()

        for k in range(2):
            hidt[c % 2, k * FH : (k + 1) * FH, :] = hid[k, c, 0].T
        xt[c % 2] = xall[c, 0, :, 0:DL].T
        for copy in keep(c):
            copy.start()

    def keep(c):
        tokens = ds(c, C)
        copies = [
            (hidt.at[c % 2], hidt_o.at[:, tokens]),
            (hid.at[0, c, 1], pg_o.at[tokens, 0:FH]),
            (hid.at[1, c, 1], pg_o.at[tokens, FH:FL]),
            (xt.at[c % 2], xt_o.at[:, tokens]),
            (xall.at[c, 1, :, 0:DL], dy_o.at[tokens, :]),
        ]
        return [pltpu.make_async_copy(*pair, hsem.at[c, i]) for i, pair in enumerate(copies)]

    def s11(c):
        for k, chunks, first in ((4, (2, 3), 0), (5, (4,), HT)):

            @pl.when(c == k)
            def _(k=k, chunks=chunks, first=first):
                for chunk in chunks:
                    got(oc.at[chunk], chunk, RX)
                half = pl.ds(first, HT)
                zs[:, half, :] = oc[OTHER, :, half, :] + xr[1, 0, :, half, :] + xr[1, 1, :, half, :] + xr[1, 2, :, half, :]
                send(zs.at[:, half, :], zr.at[:, half, :], k, RZ, ZH)

        @pl.when(c == NCH - 1)
        def _():
            for chunk in (0, 5, 6):
                got(oc.at[chunk], chunk, RX)
            for k in (4, 5):
                got(zr.at[:, 0:HT, :], k, RZ)
            for i, result in enumerate((mlp, ing)):
                total = oc[NCH - 1, i] + xr[0, 0, i] + xr[0, 1, i] + xr[0, 2, i] + zr[i]
                result[...] = total.astype(bf16)

    def s12(c):
        @pl.when(c >= NCH - 2)
        def _():
            for copy in keep(c):
                copy.wait()

        @pl.when(c != NCH - 1)
        def _():
            sent(xall.at[c, :, :, 0:DL], c, AGX)

        @pl.when((c != NCH - 1) & (c != OTHER))
        def _():
            sent(oc.at[c], c, RX)

        @pl.when((c == 4) | (c == 5))
        def _():
            sent(zr.at[:, 0:HT, :], c, RZ)

        sent(xall.at[c, :, :, 0:DL], c, AGC)
        for buf, kind in (
            (a_rel, A_REL), (a_dir, A_DIR), (a_sum, A_SUM), (a_z, A_Z),
            (b_z, B_Z), (b_rel, B_REL), (b_dir, B_DIR), (b_sum, B_SUM),
        ):
            sent(buf.at[c], c, kind)
        for rows, cols, kind in (
            (B, slice(0, WA), GA_Z), (4 * B, slice(0, WA), GA_1), (2 * B, slice(0, WA), GA_2),
            (2 * B, slice(WA, FH), GB_1), (B, slice(WA, FH), GB_2), (4 * B, slice(WA, FH), GB_Z),
        ):
            sent(hid.at[core, c, :, 0:rows, cols], c, kind)
        sent(hid.at[core, c, :, :, 0:WA], c, GC_A)
        sent(hid.at[core, c, :, :, WA:FH], c, GC_B)

    for copy in takes:
        copy.wait()
    gather()
    for copy in locals_:
        copy.start()
    for copy in swaps:
        copy.start()

    order = (
        (1, s3), (8, s10), (0, s2), (7, s9a), (7, s9b), (6, s8a), (6, s8b), (5, s7a),
        (5, s7b), (2, s4a), (2, s4b), (3, s5a), (3, s5b), (4, s6a), (4, s6b), (9, s11),
        (10, s12),
    )

    @pl.loop(0, NCH + STAGES - 1)
    def _(t):
        for stage, work in order:

            @pl.when((t >= stage) & (t < stage + NCH))
            def _(stage=stage, work=work):
                work(t - stage)

    for copy in swaps:
        copy.wait_send()


TILE = 768


def gradients(hidt, pg, xt, dy, mlp0, ing0, mlp, ing, wig, wog, gi, go, sem):
    copies = [
        pltpu.make_async_copy(mlp0, mlp, sem.at[0, 0]),
        pltpu.make_async_copy(ing0, ing, sem.at[1, 0]),
    ]
    for copy in copies:
        copy.start()
    for j in range(FL // TILE):
        units = pl.ds(j * TILE, TILE)
        go[units, :] = jnp.dot(hidt[units, :], dy[...], preferred_element_type=f32)
        gi[:, units] = jnp.dot(xt[...], pg[:, units], preferred_element_type=f32)
        for copy in (
            pltpu.make_async_copy(go.at[units, :], wog.at[units, :], sem.at[0, j + 1]),
            pltpu.make_async_copy(gi.at[:, units], wig.at[:, units], sem.at[1, j + 1]),
        ):
            copy.start()
            copies.append(copy)
    for copy in copies:
        copy.wait()


def on_device(tokens, w_in, w_out, out_grad):
    vmem, anywhere = pl.BlockSpec(memory_space=pltpu.VMEM), pl.BlockSpec(memory_space=pl.ANY)
    scratch = [
        ((NCH, 2, C, DC), bf16),
        ((DC, FH), bf16),
        ((FH, DC), bf16),
        ((DL, FL), bf16),
        ((FL, DL), bf16),
        ((NCH, 2, C, FH), bf16),
        ((NCH, 2, 2 * B, WA), bf16),
        ((NCH, 2, 2 * B, WA), bf16),
        ((NCH, 2, 2 * B, WA), bf16),
        ((NCH, 2, B, WA), bf16),
        ((NCH, 2, B, WA), bf16),
        ((NCH, 2, 4 * B, WB), bf16),
        ((NCH, 2, B, WB), bf16),
        ((NCH, 2, B, WB), bf16),
        ((NCH, 2, B, WB), bf16),
        ((2, NCH, 2, C, FH), bf16),
        ((2, FL, C), bf16),
        ((2, DL, C), bf16),
        ((NCH, 2, C, DL), f32),
        ((2, 3, 2, TOK, DL), f32),
        ((2, TOK, DL), f32),
        ((2, TOK, DL), f32),
    ]
    mlp, ing, hidt, pg, xt, dy = pl.pallas_call(
        kernel,
        out_shape=(
            pltpu.VMEM((TOK, DL), bf16),
            pltpu.VMEM((TOK, DL), bf16),
            pltpu.VMEM((FL, NCH * C), bf16),
            pltpu.VMEM((NCH * C, FL), bf16),
            pltpu.VMEM((DL, NCH * C), bf16),
            pltpu.VMEM((NCH * C, DL), bf16),
        ),
        in_specs=[anywhere] * 4,
        out_specs=(vmem, vmem, anywhere, anywhere, anywhere, anywhere),
        scratch_shapes=[pltpu.VMEM(shape, dtype) for shape, dtype in scratch]
        + [
            pltpu.SemaphoreType.DMA((NCH, KINDS)),
            pltpu.SemaphoreType.DMA((NCH, KINDS)),
            pltpu.SemaphoreType.DMA((4,)),
            pltpu.SemaphoreType.DMA((6,)),
            pltpu.SemaphoreType.DMA((NCH, 5)),
        ],
        compiler_params=pltpu.CompilerParams(
            collective_id=0, has_side_effects=True, vmem_limit_bytes=46 * 2**20
        ),
    )(tokens, out_grad, w_in, w_out)
    mlp, ing, hidt, pg, xt, dy = (
        pltpu.with_memory_space_constraint(v, pltpu.VMEM) for v in (mlp, ing, hidt, pg, xt, dy)
    )
    return pl.pallas_call(
        gradients,
        out_shape=(
            jax.ShapeDtypeStruct((TOK, DL), bf16),
            jax.ShapeDtypeStruct((TOK, DL), bf16),
            jax.ShapeDtypeStruct((DL, FL), f32),
            jax.ShapeDtypeStruct((FL, DL), f32),
        ),
        in_specs=[vmem] * 6,
        out_specs=(anywhere,) * 4,
        scratch_shapes=[
            pltpu.VMEM((DL, FL), f32),
            pltpu.VMEM((FL, DL), f32),
            pltpu.SemaphoreType.DMA((2, FL // TILE + 1)),
        ],
        compiler_params=pltpu.CompilerParams(vmem_limit_bytes=24 * 2**20),
    )(hidt, pg, xt, dy, mlp, ing)


def solution(mesh):
    in_specs = (P("row", "col"), P("col", "row"), P("row", "col"), P("row", "col"))
    out_specs = (P("row", "col"), P("row", "col"), P("col", "row"), P("row", "col"))
    return jax.shard_map(
        on_device, mesh=mesh, in_specs=in_specs, out_specs=out_specs, check_vma=False
    )
```

time: 135 us -> 127 us (0.941)
  Pallas kernels: 134 us -> 126 us
    pallas_call x2, Pallas kernels: 134 us -> 126 us  [the longest x1 119 us: on_device(): pl.pallas_call(kernel, out_shape=(pltpu.VMEM((TOK, DL), bf16), pltpu.VMEM...]
where the time goes in v3:
time: 127 us
  Pallas kernels  126 us (99%)
    pallas_call x1, Pallas kernels, on_device(): pl.pallas_call(kernel, out_shape=(pltpu.VMEM((TOK, DL), bf16), pltpu.VMEM...  119 us
    pallas_call x1, Pallas kernels, on_device(): pl.pallas_call(gradients, out_shape=(jax.ShapeDtypeStruct((TOK, DL), bf16...  6.95 us

profile of v3, /device:TPU:0, one launch (start us, length us, event | category | flops | bytes accessed | tf_op | source)
XLA Modules:
  0.0 127.0 jit_solution(6518728815000221898)
XLA Ops:
  0.6 119.4 %shard_map.75 = (bf16[128,384]{1,0:T(8,128)(2,1)S(1)}, bf16[128,384]{1,0:T(8,128)(2,1)S(1)}, bf16[3072,1024]{1,0:T(8,128)(2,1)S(1)}, bf16[1024,3072]{1,0:T(8,128...) custom-call(bf16[128,384]{1,0:T(8,128)(2,1)} %tok.1, bf16[128,384]{1,0:T(8,128)(2,1)} %dy.1, ...), custom_call_target="tpu_custom_call" | custom-call | tf_op jit(solution)/shard_map/pallas_call | solution.py:440
  120.1 7.0 %shard_map.76 = (bf16[128,384]{1,0:T(8,128)(2,1)}, bf16[128,384]{1,0:T(8,128)(2,1)}, f32[384,3072]{1,0:T(8,128)}, f32[3072,384]{1,0:T(8,128)}) custom-call(bf16[3072,1024]{1,0:T(8,128)(2,1)S(1)} %get-tuple-element.10.hidt, bf16[1024,3072]{1,0:T(8,128)(2,1)S(1)} %get-tuple-element.11.pg, bf16[384,1024]{1,0:T(8,128)(2,1)S(1)} %get-tuple-element.12.xt, ...), custom_call_target="tpu_custom_call" | custom-call | tf_op jit(solution)/shard_map/pallas_call | solution.py:467

commit v4 on v3

--- a/solution.py
+++ b/solution.py
@@ -19,13 +19,15 @@
 NCH = 8
 B = TOK // NCH
 C = B * ROWS
-WA, WB = 896, 640
+WA, WB = 1024, 512
 HA, HB = -(-WA // 256) * 128, -(-WB // 256) * 128
 HT = TOK // 2
 NEAR = {0: 0, 2: 0, 4: HT, 6: HT}
 FAR = (5, 3)
 OTHER = 1
 STAGES = 11
+FIRST, LAST = 12, 16
+HALF = NCH // 2 * C
 
 (AGX, AGC, A_REL, A_DIR, A_SUM, A_Z, B_Z, B_REL, B_DIR, B_SUM, GA_Z, GA_1, GA_2, GB_1, GB_2, GB_Z, GC_A, GC_B, RX, RZ) = range(20)
 KINDS = 20
@@ -33,11 +35,11 @@
 
 def kernel(
     tok, dy, w_in, w_out,
-    mlp, ing, hidt_o, pg_o, xt_o, dy_o,
+    mlp, ing, xt, down, hidt, grads, p_in, p_out,
     xall, wih, woh, winv, woutv, part,
     a_rel, a_dir, a_sum, a_out, a_z, b_z, b_rel, b_dir, b_sum,
-    hid, hidt, xt, oc, xr, zs, zr,
-    ssem, rsem, wsem, lsem, hsem,
+    hid, oc, xr, near6, xr6, zs, zr,
+    ssem, rsem, wsem, lsem,
 ):
     row, col = lax.axis_index("row"), lax.axis_index("col")
     x, zh = row // 2, row % 2
@@ -259,20 +261,23 @@
             for copy in locals_[2:]:
                 copy.wait()
 
+        def products(half):
+            units = ds(half, FH)
+            out = jnp.dot(hid[half, c, 0], woutv[units, :], preferred_element_type=f32)
+            back = lax.dot_general(
+                hid[half, c, 1], winv[:, units], (((1,), (1,)), ((), ())), preferred_element_type=f32
+            )
+            return out, back
+
+        oc[c, 0], oc[c, 1] = products(core)
         got(hid.at[other, c, :, :, 0:WA], c, GC_A)
         got(hid.at[other, c, :, :, WA:FH], c, GC_B)
-        for k in range(2):
-            units = pl.ds(k * FH, FH)
-            out = jnp.dot(hid[k, c, 0], woutv[units, :], preferred_element_type=f32)
-            back = lax.dot_general(
-                hid[k, c, 1], winv[:, units], (((1,), (1,)), ((), ())), preferred_element_type=f32
-            )
-            if k == 0:
-                oc[c, 0], oc[c, 1] = out, back
-            else:
-                oc[c, 0] += out
-                oc[c, 1] += back
+        out, back = products(other)
+        oc[c, 0] += out
+        oc[c, 1] += back
         for k, first in NEAR.items():
+            if k == 6:
+                continue
 
             @pl.when(c == k)
             def _(k=k, first=first):
@@ -280,33 +285,46 @@
                     dst = xr.at[int(k in (2, 4)), i, :, pl.ds(first, HT), :]
                     send(oc.at[k, :, pl.ds(i * HT, HT), :], dst, k, RX, to)
 
+        @pl.when(c == 6)
+        def _():
+            near6[...] = oc[6].astype(bf16)
+            for i, to in enumerate((XP, XM)):
+                send(near6.at[:, pl.ds(i * HT, HT), :], xr6.at[i], 6, RX, to)
+
         for k in FAR:
 
             @pl.when(c == k)
             def _(k=k):
                 send(oc.at[k], xr.at[FAR.index(k), 2], k, RX, XO)
 
-        @pl.when(c >= 2)
-        def _():
-            for copy in keep(c - 2):
-                copy.wait()
-
-        for k in range(2):
-            hidt[c % 2, k * FH : (k + 1) * FH, :] = hid[k, c, 0].T
-        xt[c % 2] = xall[c, 0, :, 0:DL].T
-        for copy in keep(c):
-            copy.start()
-
-    def keep(c):
-        tokens = ds(c, C)
-        copies = [
-            (hidt.at[c % 2], hidt_o.at[:, tokens]),
-            (hid.at[0, c, 1], pg_o.at[tokens, 0:FH]),
-            (hid.at[1, c, 1], pg_o.at[tokens, FH:FL]),
-            (xt.at[c % 2], xt_o.at[:, tokens]),
-            (xall.at[c, 1, :, 0:DL], dy_o.at[tokens, :]),
-        ]
-        return [pltpu.make_async_copy(*pair, hsem.at[c, i]) for i, pair in enumerate(copies)]
+        @pl.when(c >= NCH // 2)
+        def _():
+            tokens = ds(c - NCH // 2, C)
+            for k in range(2):
+                hidt[k * FH : (k + 1) * FH, tokens] = hid[k, c, 0].T
+                grads[tokens, k * FH : (k + 1) * FH] = hid[k, c, 1]
+            xt[:, tokens] = xall[c, 0, :, 0:DL].T
+            down[tokens, :] = xall[c, 1, :, 0:DL]
+
+    def early(t):
+        tiles = FL // 256 // (LAST - FIRST)
+        first = pl.ds(0, NCH // 2)
+        tn = (((0,), (0,)), ((), ()))
+        up_t = xall[first, 0, :, 0:DL].reshape(HALF, DL).T
+
+        @pl.loop(0, tiles)
+        def _(i):
+            j = (t - FIRST) * tiles + i
+            units, k, place = ds(j, 256), j // 6, ds(j % 6, 256)
+            p_out[units, :] = lax.dot_general(
+                hid[k, first, 0, :, place].reshape(HALF, 256),
+                xall[first, 1, :, 0:DL].reshape(HALF, DL),
+                tn,
+                preferred_element_type=f32,
+            )
+            p_in[:, units] = jnp.dot(
+                up_t, hid[k, first, 1, :, place].reshape(HALF, 256), preferred_element_type=f32
+            )
 
     def s11(c):
         for k, chunks, first in ((4, (2, 3), 0), (5, (4,), HT)):
@@ -316,32 +334,34 @@
                 for chunk in chunks:
                     got(oc.at[chunk], chunk, RX)
                 half = pl.ds(first, HT)
-                zs[:, half, :] = oc[OTHER, :, half, :] + xr[1, 0, :, half, :] + xr[1, 1, :, half, :] + xr[1, 2, :, half, :]
+                total = oc[OTHER, :, half, :] + xr[1, 2, :, half, :]
+                zs[:, half, :] = (total + xr[1, 0, :, half, :] + xr[1, 1, :, half, :]).astype(bf16)
                 send(zs.at[:, half, :], zr.at[:, half, :], k, RZ, ZH)
 
         @pl.when(c == NCH - 1)
         def _():
-            for chunk in (0, 5, 6):
+            for chunk in (0, 5):
                 got(oc.at[chunk], chunk, RX)
+            got(near6, 6, RX)
             for k in (4, 5):
                 got(zr.at[:, 0:HT, :], k, RZ)
             for i, result in enumerate((mlp, ing)):
-                total = oc[NCH - 1, i] + xr[0, 0, i] + xr[0, 1, i] + xr[0, 2, i] + zr[i]
-                result[...] = total.astype(bf16)
+                total = oc[NCH - 1, i] + xr[0, 2, i] + zr[i].astype(f32)
+                result[0:HT, :] = (total[0:HT] + xr[0, 0, i, 0:HT] + xr[0, 1, i, 0:HT]).astype(bf16)
+                result[HT:TOK, :] = (total[HT:TOK] + xr6[0, i].astype(f32) + xr6[1, i].astype(f32)).astype(bf16)
 
     def s12(c):
-        @pl.when(c >= NCH - 2)
-        def _():
-            for copy in keep(c):
-                copy.wait()
-
         @pl.when(c != NCH - 1)
         def _():
             sent(xall.at[c, :, :, 0:DL], c, AGX)
 
-        @pl.when((c != NCH - 1) & (c != OTHER))
+        @pl.when((c != NCH - 1) & (c != OTHER) & (c != 6))
         def _():
             sent(oc.at[c], c, RX)
+
+        @pl.when(c == 6)
+        def _():
+            sent(near6, 6, RX)
 
         @pl.when((c == 4) | (c == 5))
         def _():
@@ -370,13 +390,17 @@
         copy.start()
 
     order = (
-        (1, s3), (8, s10), (0, s2), (7, s9a), (7, s9b), (6, s8a), (6, s8b), (5, s7a),
-        (5, s7b), (2, s4a), (2, s4b), (3, s5a), (3, s5b), (4, s6a), (4, s6b), (9, s11),
+        (1, s3), (8, s10), (7, s9b), (7, s9a), (6, s8b), (4, s6a), (6, s8a), (0, s2),
+        (5, s7b), (5, s7a), (3, s5b), (4, s6b), (2, s4b), (9, s11), (2, s4a), (3, s5a),
         (10, s12),
     )
 
     @pl.loop(0, NCH + STAGES - 1)
     def _(t):
+        @pl.when((t >= FIRST) & (t < LAST))
+        def _():
+            early(t)
+
         for stage, work in order:
 
             @pl.when((t >= stage) & (t < stage + NCH))
@@ -390,7 +414,7 @@
 TILE = 768
 
 
-def gradients(hidt, pg, xt, dy, mlp0, ing0, mlp, ing, wig, wog, gi, go, sem):
+def gradients(mlp0, ing0, xt, down, hidt, grads, p_in, p_out, mlp, ing, wig, wog, g_in, g_out, sem):
     copies = [
         pltpu.make_async_copy(mlp0, mlp, sem.at[0, 0]),
         pltpu.make_async_copy(ing0, ing, sem.at[1, 0]),
@@ -399,11 +423,11 @@
         copy.start()
     for j in range(FL // TILE):
         units = pl.ds(j * TILE, TILE)
-        go[units, :] = jnp.dot(hidt[units, :], dy[...], preferred_element_type=f32)
-        gi[:, units] = jnp.dot(xt[...], pg[:, units], preferred_element_type=f32)
+        g_out[units, :] = p_out[units, :] + jnp.dot(hidt[units, :], down[...], preferred_element_type=f32)
+        g_in[:, units] = p_in[:, units] + jnp.dot(xt[...], grads[:, units], preferred_element_type=f32)
         for copy in (
-            pltpu.make_async_copy(go.at[units, :], wog.at[units, :], sem.at[0, j + 1]),
-            pltpu.make_async_copy(gi.at[:, units], wig.at[:, units], sem.at[1, j + 1]),
+            pltpu.make_async_copy(g_out.at[units, :], wog.at[units, :], sem.at[0, j + 1]),
+            pltpu.make_async_copy(g_in.at[:, units], wig.at[:, units], sem.at[1, j + 1]),
         ):
             copy.start()
             copies.append(copy)
@@ -430,40 +454,40 @@
         ((NCH, 2, B, WB), bf16),
         ((NCH, 2, B, WB), bf16),
         ((2, NCH, 2, C, FH), bf16),
-        ((2, FL, C), bf16),
-        ((2, DL, C), bf16),
         ((NCH, 2, C, DL), f32),
         ((2, 3, 2, TOK, DL), f32),
-        ((2, TOK, DL), f32),
-        ((2, TOK, DL), f32),
+        ((2, C, DL), bf16),
+        ((2, 2, HT, DL), bf16),
+        ((2, TOK, DL), bf16),
+        ((2, TOK, DL), bf16),
     ]
-    mlp, ing, hidt, pg, xt, dy = pl.pallas_call(
+    handed = [
+        ((TOK, DL), bf16),
+        ((TOK, DL), bf16),
+        ((DL, HALF), bf16),
+        ((HALF, DL), bf16),
+        ((FL, HALF), bf16),
+        ((HALF, FL), bf16),
+        ((DL, FL), f32),
+        ((FL, DL), f32),
+    ]
+    between = pl.pallas_call(
         kernel,
-        out_shape=(
-            pltpu.VMEM((TOK, DL), bf16),
-            pltpu.VMEM((TOK, DL), bf16),
-            pltpu.VMEM((FL, NCH * C), bf16),
-            pltpu.VMEM((NCH * C, FL), bf16),
-            pltpu.VMEM((DL, NCH * C), bf16),
-            pltpu.VMEM((NCH * C, DL), bf16),
-        ),
+        out_shape=tuple(pltpu.VMEM(shape, dtype) for shape, dtype in handed),
         in_specs=[anywhere] * 4,
-        out_specs=(vmem, vmem, anywhere, anywhere, anywhere, anywhere),
+        out_specs=(vmem,) * len(handed),
         scratch_shapes=[pltpu.VMEM(shape, dtype) for shape, dtype in scratch]
         + [
             pltpu.SemaphoreType.DMA((NCH, KINDS)),
             pltpu.SemaphoreType.DMA((NCH, KINDS)),
             pltpu.SemaphoreType.DMA((4,)),
             pltpu.SemaphoreType.DMA((6,)),
-            pltpu.SemaphoreType.DMA((NCH, 5)),
         ],
         compiler_params=pltpu.CompilerParams(
-            collective_id=0, has_side_effects=True, vmem_limit_bytes=46 * 2**20
+            collective_id=0, has_side_effects=True, vmem_limit_bytes=45 * 2**20
         ),
     )(tokens, out_grad, w_in, w_out)
-    mlp, ing, hidt, pg, xt, dy = (
-        pltpu.with_memory_space_constraint(v, pltpu.VMEM) for v in (mlp, ing, hidt, pg, xt, dy)
-    )
+    between = [pltpu.with_memory_space_constraint(v, pltpu.VMEM) for v in between]
     return pl.pallas_call(
         gradients,
         out_shape=(
@@ -472,15 +496,15 @@
             jax.ShapeDtypeStruct((DL, FL), f32),
             jax.ShapeDtypeStruct((FL, DL), f32),
         ),
-        in_specs=[vmem] * 6,
+        in_specs=[vmem] * len(handed),
         out_specs=(anywhere,) * 4,
         scratch_shapes=[
             pltpu.VMEM((DL, FL), f32),
             pltpu.VMEM((FL, DL), f32),
             pltpu.SemaphoreType.DMA((2, FL // TILE + 1)),
         ],
-        compiler_params=pltpu.CompilerParams(vmem_limit_bytes=24 * 2**20),
-    )(hidt, pg, xt, dy, mlp, ing)
+        compiler_params=pltpu.CompilerParams(vmem_limit_bytes=12 * 2**20),
+    )(*between)
 
 
 def solution(mesh):

time: 127 us -> 123 us (0.969)
  Pallas kernels: 126 us -> 122 us
    pallas_call x1, Pallas kernels: 6.95 us -> 4.34 us  [on_device(): pl.pallas_call(gradients, out_shape=(jax.ShapeDtypeStruct((TOK, DL), bf16...]
    pallas_call x1, Pallas kernels: 119 us -> 118 us  [on_device(): pl.pallas_call(kernel, out_shape=tuple((pltpu.VMEM(shape, dtype) for shap...]
where the time goes in v4:
time: 123 us
  Pallas kernels  122 us (99%)
    pallas_call x1, Pallas kernels, on_device(): pl.pallas_call(kernel, out_shape=tuple((pltpu.VMEM(shape, dtype) for shap...  118 us
    pallas_call x1, Pallas kernels, on_device(): pl.pallas_call(gradients, out_shape=(jax.ShapeDtypeStruct((TOK, DL), bf16...  4.34 us

profile of v4, /device:TPU:0, one launch (start us, length us, event | category | flops | bytes accessed | tf_op | source)
XLA Modules:
  0.0 122.8 jit_solution(13680027109304310213)
XLA Ops:
  0.6 117.8 %shard_map.75 = (bf16[128,384]{1,0:T(8,128)(2,1)S(1)}, bf16[128,384]{1,0:T(8,128)(2,1)S(1)}, bf16[384,512]{1,0:T(8,128)(2,1)S(1)}, bf16[512,384]{1,0:T(8,128)(2,...) custom-call(bf16[128,384]{1,0:T(8,128)(2,1)} %tok.1, ...), custom_call_target="tpu_custom_call" | custom-call | tf_op jit(solution)/shard_map/pallas_call | solution.py:474
  118.5 4.3 %shard_map.76 = (bf16[128,384]{1,0:T(8,128)(2,1)}, bf16[128,384]{1,0:T(8,128)(2,1)}, f32[384,3072]{1,0:T(8,128)}, f32[3072,384]{1,0:T(8,128)}) custom-call(bf16[128,384]{1,0:T(8,128)(2,1)S(1)} %get-tuple-element.12.mlp0, bf16[128,384]{1,0:T(8,128)(2,1)S(1)} %get-tuple-element.13.ing0, bf16[384,512]{1,0:T(8,128)(2,1)S(1)} %get-tuple-element.14.xt, ...), custom_call_target="tpu_custom_call" | custom-call | tf_op jit(solution)/shard_map/pallas_call | solution.py:491

commit v5 on v4

--- a/solution.py
+++ b/solution.py
@@ -26,7 +26,7 @@
 FAR = (5, 3)
 OTHER = 1
 STAGES = 11
-FIRST, LAST = 12, 16
+FIRST, LAST = 11, 15
 HALF = NCH // 2 * C
 
 (AGX, AGC, A_REL, A_DIR, A_SUM, A_Z, B_Z, B_REL, B_DIR, B_SUM, GA_Z, GA_1, GA_2, GB_1, GB_2, GB_Z, GC_A, GC_B, RX, RZ) = range(20)
@@ -384,14 +384,14 @@
     for copy in takes:
         copy.wait()
     gather()
+    for copy in swaps:
+        copy.start()
     for copy in locals_:
         copy.start()
-    for copy in swaps:
-        copy.start()
 
     order = (
-        (1, s3), (8, s10), (7, s9b), (7, s9a), (6, s8b), (4, s6a), (6, s8a), (0, s2),
-        (5, s7b), (5, s7a), (3, s5b), (4, s6b), (2, s4b), (9, s11), (2, s4a), (3, s5a),
+        (9, s11), (7, s9a), (7, s9b), (6, s8a), (5, s7a), (6, s8b), (7, s10), (1, s3),
+        (0, s2), (5, s7b), (4, s6a), (4, s6b), (2, s4b), (2, s4a), (3, s5a), (3, s5b),
         (10, s12),
     )
 
@@ -411,7 +411,7 @@
         copy.wait_send()
 
 
-TILE = 768
+TILE = 512
 
 
 def gradients(mlp0, ing0, xt, down, hidt, grads, p_in, p_out, mlp, ing, wig, wog, g_in, g_out, sem):

time: 123 us -> 121 us (0.984)
  Pallas kernels: 122 us -> 120 us
    pallas_call x1, Pallas kernels: 118 us -> 115 us  [on_device(): pl.pallas_call(kernel, out_shape=tuple((pltpu.VMEM(shape, dtype) for shap...]
where the time goes in v5:
time: 121 us; the launch traced here: 120 us
  Pallas kernels  120 us (99%)
    pallas_call x1, Pallas kernels, on_device(): pl.pallas_call(kernel, out_shape=tuple((pltpu.VMEM(shape, dtype) for shap...  115 us
    pallas_call x1, Pallas kernels, on_device(): pl.pallas_call(gradients, out_shape=(jax.ShapeDtypeStruct((TOK, DL), bf16...  4.18 us

profile of v5, /device:TPU:0, one launch (start us, length us, event | category | flops | bytes accessed | tf_op | source)
XLA Modules:
  0.0 120.3 jit_solution(17684868672358231777)
XLA Ops:
  0.6 115.5 %shard_map.75 = (bf16[128,384]{1,0:T(8,128)(2,1)S(1)}, bf16[128,384]{1,0:T(8,128)(2,1)S(1)}, bf16[384,512]{1,0:T(8,128)(2,1)S(1)}, bf16[512,384]{1,0:T(8,128)(2,...) custom-call(bf16[128,384]{1,0:T(8,128)(2,1)} %tok.1, ...), custom_call_target="tpu_custom_call" | custom-call | tf_op jit(solution)/shard_map/pallas_call | solution.py:474
  116.1 4.2 %shard_map.76 = (bf16[128,384]{1,0:T(8,128)(2,1)}, bf16[128,384]{1,0:T(8,128)(2,1)}, f32[384,3072]{1,0:T(8,128)}, f32[3072,384]{1,0:T(8,128)}) custom-call(bf16[128,384]{1,0:T(8,128)(2,1)S(1)} %get-tuple-element.12.mlp0, bf16[128,384]{1,0:T(8,128)(2,1)S(1)} %get-tuple-element.13.ing0, bf16[384,512]{1,0:T(8,128)(2,1)S(1)} %get-tuple-element.14.xt, ...), custom_call_target="tpu_custom_call" | custom-call | tf_op jit(solution)/shard_map/pallas_call | solution.py:491

commit v6 on v5

--- a/solution.py
+++ b/solution.py
@@ -25,7 +25,7 @@
 NEAR = {0: 0, 2: 0, 4: HT, 6: HT}
 FAR = (5, 3)
 OTHER = 1
-STAGES = 11
+STAGES = 10
 FIRST, LAST = 11, 15
 HALF = NCH // 2 * C
 
@@ -326,31 +326,7 @@
                 up_t, hid[k, first, 1, :, place].reshape(HALF, 256), preferred_element_type=f32
             )
 
-    def s11(c):
-        for k, chunks, first in ((4, (2, 3), 0), (5, (4,), HT)):
-
-            @pl.when(c == k)
-            def _(k=k, chunks=chunks, first=first):
-                for chunk in chunks:
-                    got(oc.at[chunk], chunk, RX)
-                half = pl.ds(first, HT)
-                total = oc[OTHER, :, half, :] + xr[1, 2, :, half, :]
-                zs[:, half, :] = (total + xr[1, 0, :, half, :] + xr[1, 1, :, half, :]).astype(bf16)
-                send(zs.at[:, half, :], zr.at[:, half, :], k, RZ, ZH)
-
-        @pl.when(c == NCH - 1)
-        def _():
-            for chunk in (0, 5):
-                got(oc.at[chunk], chunk, RX)
-            got(near6, 6, RX)
-            for k in (4, 5):
-                got(zr.at[:, 0:HT, :], k, RZ)
-            for i, result in enumerate((mlp, ing)):
-                total = oc[NCH - 1, i] + xr[0, 2, i] + zr[i].astype(f32)
-                result[0:HT, :] = (total[0:HT] + xr[0, 0, i, 0:HT] + xr[0, 1, i, 0:HT]).astype(bf16)
-                result[HT:TOK, :] = (total[HT:TOK] + xr6[0, i].astype(f32) + xr6[1, i].astype(f32)).astype(bf16)
-
-    def s12(c):
+    def settle(c):
         @pl.when(c != NCH - 1)
         def _():
             sent(xall.at[c, :, :, 0:DL], c, AGX)
@@ -363,9 +339,9 @@
         def _():
             sent(near6, 6, RX)
 
-        @pl.when((c == 4) | (c == 5))
-        def _():
-            sent(zr.at[:, 0:HT, :], c, RZ)
+        @pl.when((c == 5) | (c == 6))
+        def _():
+            sent(zr.at[:, 0:HT, :], c - 1, RZ)
 
         sent(xall.at[c, :, :, 0:DL], c, AGC)
         for buf, kind in (
@@ -380,6 +356,36 @@
             sent(hid.at[core, c, :, 0:rows, cols], c, kind)
         sent(hid.at[core, c, :, :, 0:WA], c, GC_A)
         sent(hid.at[core, c, :, :, WA:FH], c, GC_B)
+
+    def s12(c):
+        pl.when(c < NCH - 2)(lambda: settle(c))
+
+    def s11(c):
+        for k, chunks, first in ((4, (2, 3), 0), (5, (4,), HT)):
+
+            @pl.when(c == k)
+            def _(k=k, chunks=chunks, first=first):
+                for chunk in chunks:
+                    got(oc.at[chunk], chunk, RX)
+                half = pl.ds(first, HT)
+                total = oc[OTHER, :, half, :] + xr[1, 2, :, half, :]
+                zs[:, half, :] = (total + xr[1, 0, :, half, :] + xr[1, 1, :, half, :]).astype(bf16)
+                send(zs.at[:, half, :], zr.at[:, half, :], k, RZ, ZH)
+
+        @pl.when(c == NCH - 1)
+        def _():
+            pl.loop(NCH - 2, NCH)(settle)
+            for chunk in (0, 5):
+                got(oc.at[chunk], chunk, RX)
+            for k in (4, 5):
+                got(zr.at[:, 0:HT, :], k, RZ)
+            totals = [oc[NCH - 1, i] + xr[0, 2, i] + zr[i].astype(f32) for i in range(2)]
+            for i, result in enumerate((mlp, ing)):
+                result[0:HT, :] = (totals[i][0:HT] + xr[0, 0, i, 0:HT] + xr[0, 1, i, 0:HT]).astype(bf16)
+            got(near6, 6, RX)
+            for i, result in enumerate((mlp, ing)):
+                both = xr6[0, i].astype(f32) + xr6[1, i].astype(f32)
+                result[HT:TOK, :] = (totals[i][HT:TOK] + both).astype(bf16)
 
     for copy in takes:
         copy.wait()

time: 121 us -> 121 us (level)
  no operation moved by 1% of the time
where the time goes in v6:
time: 121 us; the launch traced here: 120 us
  Pallas kernels  119 us (98%)
    pallas_call x1, Pallas kernels, on_device(): pl.pallas_call(kernel, out_shape=tuple((pltpu.VMEM(shape, dtype) for shap...  115 us
    pallas_call x1, Pallas kernels, on_device(): pl.pallas_call(gradients, out_shape=(jax.ShapeDtypeStruct((TOK, DL), bf16...  4.18 us

profile of v6, /device:TPU:0, one launch (start us, length us, event | category | flops | bytes accessed | tf_op | source)
XLA Modules:
  0.0 120.1 jit_solution(6749956585942774702)
XLA Ops:
  0.6 115.3 %shard_map.75 = (bf16[128,384]{1,0:T(8,128)(2,1)S(1)}, bf16[128,384]{1,0:T(8,128)(2,1)S(1)}, bf16[384,512]{1,0:T(8,128)(2,1)S(1)}, bf16[512,384]{1,0:T(8,128)(2,...) custom-call(bf16[128,384]{1,0:T(8,128)(2,1)} %tok.1, ...), custom_call_target="tpu_custom_call" | custom-call | tf_op jit(solution)/shard_map/pallas_call | solution.py:480
  115.9 4.2 %shard_map.76 = (bf16[128,384]{1,0:T(8,128)(2,1)}, bf16[128,384]{1,0:T(8,128)(2,1)}, f32[384,3072]{1,0:T(8,128)}, f32[3072,384]{1,0:T(8,128)}) custom-call(bf16[128,384]{1,0:T(8,128)(2,1)S(1)} %get-tuple-element.12.mlp0, bf16[128,384]{1,0:T(8,128)(2,1)S(1)} %get-tuple-element.13.ing0, bf16[384,512]{1,0:T(8,128)(2,1)S(1)} %get-tuple-element.14.xt, ...), custom_call_target="tpu_custom_call" | custom-call | tf_op jit(solution)/shard_map/pallas_call | solution.py:497

commit v7 on v6

--- a/solution.py
+++ b/solution.py
@@ -79,7 +79,13 @@
     takes = [
         pltpu.make_async_copy(src, xall.at[NCH - 1, i, :, 0:DL], lsem.at[4 + i]) for i, src in enumerate((tok, dy))
     ]
-    for copy in takes:
+    locals_ = [
+        pltpu.make_async_copy(w_in.at[:, ds(core, FH)], wih.at[pl.ds(0, DL), :], lsem.at[0]),
+        pltpu.make_async_copy(w_out.at[ds(core, FH), :], woh.at[:, pl.ds(0, DL)], lsem.at[1]),
+        pltpu.make_async_copy(w_in, winv, lsem.at[2]),
+        pltpu.make_async_copy(w_out, woutv, lsem.at[3]),
+    ]
+    for copy in takes + locals_:
         copy.start()
     pl.semaphore_wait(barrier, 8)
 
@@ -92,12 +98,6 @@
             src_ref=w_out.at[ds(other, FH), :], dst_ref=woh.at[:, pl.ds(DL, DL)],
             send_sem=wsem.at[2], recv_sem=wsem.at[3], device_id=CO, device_id_type=MESH,
         ),
-    ]
-    locals_ = [
-        pltpu.make_async_copy(w_in.at[:, ds(core, FH)], wih.at[pl.ds(0, DL), :], lsem.at[0]),
-        pltpu.make_async_copy(w_out.at[ds(core, FH), :], woh.at[:, pl.ds(0, DL)], lsem.at[1]),
-        pltpu.make_async_copy(w_in, winv, lsem.at[2]),
-        pltpu.make_async_copy(w_out, woutv, lsem.at[3]),
     ]
     def near(c, src):
         half = pl.ds(NEAR[c], HT)
@@ -391,8 +391,6 @@
         copy.wait()
     gather()
     for copy in swaps:
-        copy.start()
-    for copy in locals_:
         copy.start()
 
     order = (

time: 121 us -> 121 us (level)
  no operation moved by 1% of the time
where the time goes in v7:
time: 121 us; the launch traced here: 120 us
  Pallas kernels  119 us (98%)
    pallas_call x1, Pallas kernels, on_device(): pl.pallas_call(kernel, out_shape=tuple((pltpu.VMEM(shape, dtype) for shap...  115 us
    pallas_call x1, Pallas kernels, on_device(): pl.pallas_call(gradients, out_shape=(jax.ShapeDtypeStruct((TOK, DL), bf16...  4.18 us

profile of v7, /device:TPU:0, one launch (start us, length us, event | category | flops | bytes accessed | tf_op | source)
XLA Modules:
  0.0 120.1 jit_solution(7567544574790862708)
XLA Ops:
  0.6 115.3 %shard_map.75 = (bf16[128,384]{1,0:T(8,128)(2,1)S(1)}, bf16[128,384]{1,0:T(8,128)(2,1)S(1)}, bf16[384,512]{1,0:T(8,128)(2,1)S(1)}, bf16[512,384]{1,0:T(8,128)(2,...) custom-call(bf16[128,384]{1,0:T(8,128)(2,1)} %tok.1, ...), custom_call_target="tpu_custom_call" | custom-call | tf_op jit(solution)/shard_map/pallas_call | solution.py:478
  115.9 4.2 %shard_map.76 = (bf16[128,384]{1,0:T(8,128)(2,1)}, bf16[128,384]{1,0:T(8,128)(2,1)}, f32[384,3072]{1,0:T(8,128)}, f32[3072,384]{1,0:T(8,128)}) custom-call(bf16[128,384]{1,0:T(8,128)(2,1)S(1)} %get-tuple-element.12.mlp0, bf16[128,384]{1,0:T(8,128)(2,1)S(1)} %get-tuple-element.13.ing0, bf16[384,512]{1,0:T(8,128)(2,1)S(1)} %get-tuple-element.14.xt, ...), custom_call_target="tpu_custom_call" | custom-call | tf_op jit(solution)/shard_map/pallas_call | solution.py:495
